TPU v7x, 32 devices: a whole 2x2x4 slice. The times are simulated.
32 devices in a mesh: slab: 16 (over z, x, core), band: 2 (over y).
Axes of the slice: x: 2, y: 2, z: 4, core: 2. Of those that a mesh axis runs over, the one named last changes fastest.
Arguments:
- hamiltonian: bfloat16 [128, 7, 128, 128], P('slab', None, 'band'), may hold values from -0.1875 to 0.1875
- neighbors: int32 [128, 7], P('slab'), may hold values from 0 to 11, as said below
- orbitals: bfloat16 [16384, 1024], P('slab', 'band'), may hold values from -6 to 6
Outputs:
- residual: bfloat16 [16384, 1024], P(('slab', 'band'))
Inputs may be any that keep to these rules, and one draw needn't show every extreme that they name: `neighbors`: window positions 0 to 1 are the last 2 elements of the slab below (periodic), 2 to 9 the slab's own elements, the rest the first 2 elements of the slab above. A slab's elements are in layers of 2; each block row names, in an order of its own, itself, the element 2 positions below and above it in the window, and four elements of its own layer (repeats possible).
All inputs are finite; a program needn't handle non-finite values.
Results may differ from a plain program's by a relative error of at most 0.012.
Values may be sent and summed in bfloat16 or wider, within the bound.
A program may use at most 64 MiB of HBM per device.

v0:
```python
import math

import jax
import jax.numpy as jnp
from jax import lax
from jax.sharding import PartitionSpec as P

FACE = 2


def padded(block, sides, width):
    for axis, dim in sides:
        count = lax.axis_size(axis)
        forward = [(i, i + 1) for i in range(count - 1)]
        forward.append((count - 1, 0))
        backward = [(target, source) for source, target in forward]
        low = lax.ppermute(
            lax.slice_in_dim(block, block.shape[dim] - width, None, axis=dim), axis, forward
        )
        high = lax.ppermute(lax.slice_in_dim(block, 0, width, axis=dim), axis, backward)
        block = jnp.concatenate([low, block, high], axis=dim)
    return block


def apply_local(vector, full_tiles, neighbors):
    tile_size = full_tiles.shape[2]
    extended = padded(vector, (("slab", 0),), FACE * tile_size)
    blocks = extended.reshape(-1, tile_size, vector.shape[1])
    picked_blocks = blocks[neighbors]
    product = jnp.einsum(
        "rjab,rjbc->rac", full_tiles, picked_blocks, preferred_element_type=jnp.float32
    )
    return product.reshape(vector.shape[0], vector.shape[1])


def body(hamiltonian, neighbors, orbitals):
    full_tiles = lax.all_gather(hamiltonian, "band", axis=2, tiled=True)
    first = apply_local(orbitals, full_tiles, neighbors).astype(jnp.bfloat16)
    second = (
        2.0 * apply_local(first, full_tiles, neighbors) - orbitals.astype(jnp.float32)
    ).astype(jnp.bfloat16)
    third = (2.0 * apply_local(second, full_tiles, neighbors) - first.astype(jnp.float32)).astype(
        jnp.bfloat16
    )
    applied = apply_local(third, full_tiles, neighbors).astype(jnp.bfloat16)
    rows_all = orbitals.shape[0] * lax.axis_size("slab")
    bands_all = orbitals.shape[1] * lax.axis_size("band")
    gram_scale = 1.0 / math.sqrt(float(rows_all) * float(bands_all))
    strip_third, strip_applied = (
        lax.all_to_all(third, "band", split_axis=0, concat_axis=1, tiled=True),
        lax.all_to_all(applied, "band", split_axis=0, concat_axis=1, tiled=True),
    )
    columns = strip_third
    row_block = lax.psum_scatter(
        jnp.einsum("rb,rc->bc", columns, strip_applied, preferred_element_type=jnp.float32).astype(
            jnp.bfloat16
        ),
        "band",
        scatter_dimension=0,
        tiled=True,
    ).astype(jnp.float32)
    slab_summed = lax.psum(row_block, "slab")
    gram_block = (slab_summed * gram_scale).astype(jnp.bfloat16)
    columns = strip_third
    mixed = jnp.dot(
        columns,
        lax.all_gather(gram_block, "band", axis=0, tiled=True),
        preferred_element_type=jnp.float32,
    )
    return (strip_applied.astype(jnp.float32) - mixed).astype(jnp.bfloat16)


def solution(mesh):
    in_specs = (P("slab", None, "band", None), P("slab", None), P("slab", "band"))
    out_specs = P(("slab", "band"), None)
    return jax.shard_map(body, mesh=mesh, in_specs=in_specs, out_specs=out_specs, check_vma=False)
```

profile of v0, /device:TPU:1, one launch (start us, length us, event | category | flops | bytes accessed | tf_op | source)
XLA Modules:
  0.0 288.7 jit_solution(16987525623396219544)
XLA Ops:
  8.3 2.7 collective-permute-start
  11.8 2.5 collective-permute-done
  14.3 5.3 %collective-permute-done.1 = bf16[256,512]{1,0:T(8,128)(2,1)S(1)} collective-permute-done((bf16[256,512]{1,0:T(8,128)(2,1)S(1)}, bf16[256,512]{1,0:T(8,128)(2,1)S(1)}, u32[]{:S(2)}, u32[]{:S(2)}) %collective-permute-start.1) | collective-permute-done | bytes 262176 | tf_op jit(solution)/shard_map/ppermute | solution.py:20
  19.7 5.3 %gather_fusion = bf16[56,128,512]{2,1,0:T(8,128)(2,1)} fusion(bf16[12,128,512]{2,1,0:T(8,128)(2,1)S(1)} %bitcast.64, s32[1024]{0:T(1024)S(1)} %pad_clamp_fusion), kind=kCustom, calls=%fused_computation | custom fusion | bytes 14680288 | tf_op jit(solution)/shard_map/gather | solution.py:29
  25.0 16.2 %all-gather.3.cloned.1.call-done = bf16[8,7,128,128]{3,2,1,0:T(8,128)(2,1)} async-done(((bf16[8,7,64,128]{3,2,1,0:T(8,128)(2,1)}), bf16[8,7,128,128]{3,2,1,0:T(8,128)(2,1)}) %all-gather.3.cloned.1.call-update) | async-done | bytes 1835024 | tf_op jit(solution)/shard_map/all_gather | solution.py:37
  41.2 4.9 %bitcast_convert_fusion.1 = bf16[8,512,128]{1,2,0:T(8,128)(2,1)S(1)} fusion(bf16[8,7,128,128]{3,2,1,0:T(8,128)(2,1)} %all-gather.3.cloned.1.call-done, bf16[8,7,128,512]{3,2,1,0:T(8,128)(2,1)} %bitcast.67), kind=kOutput, calls=%fused_computation.11 | convolution fusion | flops 940048384 | bytes 10223616 | tf_op jit(solution)/shard_map/rjab,rjbc->rac/dot_general | solution.py:30
  46.9 1.1 collective-permute-start.2
  48.0 4.0 %collective-permute-done.3 = bf16[256,512]{1,0:T(8,128)(2,1)S(1)} collective-permute-done((bf16[256,512]{1,0:T(8,128)(2,1)S(1)}, bf16[256,512]{1,0:T(8,128)(2,1)S(1)}, u32[]{:S(2)}, u32[]{:S(2)}) %collective-permute-start.3) | collective-permute-done | bytes 262176 | tf_op jit(solution)/shard_map/ppermute | solution.py:20
  52.0 2.1 collective-permute-done.2
  54.3 5.3 %gather_fusion.1 = bf16[56,128,512]{2,1,0:T(8,128)(2,1)} fusion(bf16[12,128,512]{2,1,0:T(8,128)(2,1)S(1)} %bitcast.65, s32[1024]{0:T(1024)S(1)} %pad_clamp_fusion), kind=kCustom, calls=%fused_computation.1 | custom fusion | bytes 14680288 | tf_op jit(solution)/shard_map/gather | solution.py:29
  59.5 4.4 %bitcast_multiply_fusion.1 = f32[8,512,128]{1,2,0:T(8,128)S(1)} fusion(bf16[8,7,128,128]{3,2,1,0:T(8,128)(2,1)S(1)} %copy-done, bf16[8,7,128,512]{3,2,1,0:T(8,128)(2,1)} %bitcast.69), kind=kOutput, calls=%fused_computation.10 | convolution fusion | flops 940048384 | bytes 11272192 | tf_op jit(solution)/shard_map/rjab,rjbc->rac/dot_general | solution.py:30
  64.4 2.5 collective-permute-start.4
  66.9 2.5 collective-permute-start.5
  69.4 3.6 %collective-permute-done.4 = bf16[256,512]{1,0:T(8,128)(2,1)S(1)} collective-permute-done((bf16[256,512]{1,0:T(8,128)(2,1)S(1)}, bf16[256,512]{1,0:T(8,128)(2,1)S(1)}, u32[]{:S(2)}, u32[]{:S(2)}) %collective-permute-start.4) | collective-permute-done | bytes 262176 | tf_op jit(solution)/shard_map/ppermute | solution.py:17
  73.2 5.3 %gather_fusion.2 = bf16[56,128,512]{2,1,0:T(8,128)(2,1)} fusion(bf16[12,128,512]{2,1,0:T(8,128)(2,1)S(1)} %bitcast.63, s32[1024]{0:T(1024)S(1)} %pad_clamp_fusion), kind=kCustom, calls=%fused_computation.2 | custom fusion | bytes 14680288 | tf_op jit(solution)/shard_map/gather | solution.py:29
  78.4 5.7 %subtract_convert_fusion.1 = (bf16[8,512,128]{1,2,0:T(8,128)(2,1)}, f32[8,512,128]{1,2,0:T(8,128)S(1)}) fusion(bf16[8,512,128]{1,2,0:T(8,128)(2,1)} %copy-done.1, bf16[8,7,128,128]{3,2,1,0:T(8,128)(2,1)S(1)} %copy-done, bf16[8,7,128,512]{3,2,1,0:T(8,128)(2,1)} %bitcast.66), kind=kOutput, calls=%fused_computation.14 | convolution fusion | flops 941621248 | bytes 13369344 | tf_op jit(solution)/shard_map/rjab,rjbc->rac/dot_general | solution.py:30
  84.6 2.5 collective-permute-start.6
  87.2 2.4 collective-permute-start.7
  89.6 3.7 %collective-permute-done.6 = bf16[256,512]{1,0:T(8,128)(2,1)S(1)} collective-permute-done((bf16[256,512]{1,0:T(8,128)(2,1)S(1)}, bf16[256,512]{1,0:T(8,128)(2,1)S(1)}, u32[]{:S(2)}, u32[]{:S(2)}) %collective-permute-start.6) | collective-permute-done | bytes 262176 | tf_op jit(solution)/shard_map/ppermute | solution.py:17
  93.4 5.3 %gather_fusion.3 = bf16[56,128,512]{2,1,0:T(8,128)(2,1)} fusion(bf16[12,128,512]{2,1,0:T(8,128)(2,1)S(1)} %bitcast.62, s32[1024]{0:T(1024)S(1)} %pad_clamp_fusion), kind=kCustom, calls=%fused_computation.3 | custom fusion | bytes 14680288 | tf_op jit(solution)/shard_map/gather | solution.py:29
  98.6 5.3 %bitcast_convert_fusion = bf16[8,512,128]{1,2,0:T(8,128)(2,1)} fusion(bf16[8,7,128,128]{3,2,1,0:T(8,128)(2,1)S(1)} %copy-done, bf16[8,7,128,512]{3,2,1,0:T(8,128)(2,1)} %bitcast.68), kind=kOutput, calls=%fused_computation.8 | convolution fusion | flops 940048384 | bytes 10223616 | tf_op jit(solution)/shard_map/rjab,rjbc->rac/dot_general | solution.py:30
  103.9 3.7 %all-to-all-start = ((bf16[2,512,512]{2,1,0:T(8,128)(2,1)}), bf16[2,512,512]{2,1,0:T(8,128)(2,1)S(1)}, u32[]{:S(2)}, u32[]{:S(2)}) async-start(bf16[2,512,512]{2,1,0:T(8,128)(2,1)} %bitcast.26), calls=%async_computation | async-start | bytes 2097152 | tf_op jit(solution)/shard_map/all_to_all | solution.py:51
  107.7 1.3 copy.6
  109.0 7.5 %all-to-all-done = bf16[2,512,512]{2,1,0:T(8,128)(2,1)S(1)} async-done(((bf16[2,512,512]{2,1,0:T(8,128)(2,1)}), bf16[2,512,512]{2,1,0:T(8,128)(2,1)S(1)}, u32[]{:S(2)}, u32[]{:S(2)}) %all-to-all-start) | async-done | bytes 1048608 | tf_op jit(solution)/shard_map/all_to_all | solution.py:51
  116.5 3.6 %all-to-all-start.1 = ((bf16[2,512,512]{1,2,0:T(8,128)(2,1)}), bf16[2,512,512]{1,2,0:T(8,128)(2,1)S(1)}, u32[]{:S(2)}, u32[]{:S(2)}) async-start(bf16[2,512,512]{1,2,0:T(8,128)(2,1)} %copy.6), calls=%async_computation.1 | async-start | bytes 2097152 | tf_op jit(solution)/shard_map/all_to_all | solution.py:50
  120.5 7.8 %all-to-all-done.1 = bf16[2,512,512]{1,2,0:T(8,128)(2,1)S(1)} async-done(((bf16[2,512,512]{1,2,0:T(8,128)(2,1)}), bf16[2,512,512]{1,2,0:T(8,128)(2,1)S(1)}, u32[]{:S(2)}, u32[]{:S(2)}) %all-to-all-start.1) | async-done | bytes 1048608 | tf_op jit(solution)/shard_map/all_to_all | solution.py:50
  128.3 2.6 convolution_convert_fusion
  131.0 40.6 %reduce-scatter.2.cloned.1.call-done = bf16[512,1024]{1,0:T(8,128)(2,1)} async-done(((bf16[1024,1024]{1,0:T(8,128)(2,1)}), bf16[512,1024]{1,0:T(8,128)(2,1)}) %reduce-scatter.2.cloned.1.call-update) | async-done | bytes 1048592 | tf_op jit(solution)/shard_map/reduce_scatter | solution.py:54
  171.6 71.1 %all-reduce.1 = f32[512,1024]{1,0:T(8,128)S(1)} all-reduce(bf16[512,1024]{1,0:T(8,128)(2,1)} %reduce-scatter.2.cloned.1.call-done), channel_id=1, replica_groups=mesh['slab'=16,'band'=2] {'slab'}, use_global_device_ids=true, to_apply=%region_1.0 | all-reduce | flops 524288 | bytes 3145728 | tf_op jit(solution)/shard_map/psum | solution.py:62
  242.7 1.3 multiply_convert_fusion
  244.0 34.1 %all-gather.5.cloned.1.call-done = bf16[1024,1024]{1,0:T(8,128)(2,1)} async-done(((bf16[512,1024]{1,0:T(8,128)(2,1)}), bf16[1024,1024]{1,0:T(8,128)(2,1)}) %all-gather.5.cloned.1.call-update) | async-done | bytes 2097168 | tf_op jit(solution)/shard_map/all_gather | solution.py:67
  278.1 4.1 %subtract_convert_fusion = bf16[512,1024]{1,0:T(8,128)(2,1)} fusion(bf16[512,1024]{1,0:T(8,128)(2,1)} %bitcast.77, bf16[512,1024]{0,1:T(8,128)(2,1)S(1)} %bitcast.75, bf16[1024,1024]{1,0:T(8,128)(2,1)} %all-gather.5.cloned.1.call-done), kind=kOutput, calls=%fused_computation.12 | convolution fusion | flops 1075314688 | bytes 5242880 | tf_op jit(solution)/shard_map/dot_general | solution.py:65
  (38 shorter events, 5.1 us)
Async XLA Ops:
  6.5 13.1 %copy-start.3 = (bf16[1024,512]{1,0:T(8,128)(2,1)S(1)}, bf16[1024,512]{1,0:T(8,128)(2,1)}, u32[]{:S(2)}) copy-start(bf16[1024,512]{1,0:T(8,128)(2,1)} %param.5) | copy-start | bytes 3145732
  6.5 34.6 %all-gather.3.cloned.1.call-start = ((), (), s32[]{:S(2)}) async-start(), calls=%async_computation.3 | async-start | bytes 2752512 | tf_op jit(solution)/shard_map/all_gather | solution.py:37
  8.3 6.0 %collective-permute-start = (bf16[256,512]{1,0:T(8,128)(2,1)S(1)}, bf16[256,512]{1,0:T(8,128)(2,1)S(1)}, u32[]{:S(2)}, u32[]{:S(2)}) collective-permute-start(bf16[256,512]{1,0:T(8,128)(2,1)S(1)} %get-tuple-element.11), channel_id=1, source_target_pairs={{0,2},{2,4},{4,6},{6,8},{8,10},{10,12},{12,14},{14,16},{16,18},{18... | collective-permute-start | bytes 786440 | tf_op jit(solution)/shard_map/ppermute | solution.py:17
  11.0 8.6 %collective-permute-start.1 = (bf16[256,512]{1,0:T(8,128)(2,1)S(1)}, bf16[256,512]{1,0:T(8,128)(2,1)S(1)}, u32[]{:S(2)}, u32[]{:S(2)}) collective-permute-start(bf16[256,512]{1,0:T(8,128)(2,1)S(1)} %get-tuple-element.12), channel_id=1, source_target_pairs={{2,0},{4,2},{6,4},{8,6},{10,8},{12,10},{14,12},{16,14},{18,16},{20... | collective-permute-start | bytes 786440 | tf_op jit(solution)/shard_map/ppermute | solution.py:20
  46.1 8.2 %copy-start.1 = (bf16[8,512,128]{1,2,0:T(8,128)(2,1)}, bf16[8,512,128]{1,2,0:T(8,128)(2,1)S(1)}, u32[]{:S(2)}) copy-start(bf16[8,512,128]{1,2,0:T(8,128)(2,1)S(1)} %bitcast_convert_fusion.1) | copy-start | bytes 3145732
  46.1 5.9 %collective-permute-start.3 = (bf16[256,512]{1,0:T(8,128)(2,1)S(1)}, bf16[256,512]{1,0:T(8,128)(2,1)S(1)}, u32[]{:S(2)}, u32[]{:S(2)}) collective-permute-start(bf16[256,512]{1,0:T(8,128)(2,1)S(1)} %bitcast.79), channel_id=1, source_target_pairs={{2,0},{4,2},{6,4},{8,6},{10,8},{12,10},{14,12},{16,14},{18,16},{20... | collective-permute-start | bytes 786440 | tf_op jit(solution)/shard_map/ppermute | solution.py:20
  46.9 7.3 %collective-permute-start.2 = (bf16[256,512]{1,0:T(8,128)(2,1)S(1)}, bf16[256,512]{1,0:T(8,128)(2,1)S(1)}, u32[]{:S(2)}, u32[]{:S(2)}) collective-permute-start(bf16[256,512]{1,0:T(8,128)(2,1)S(1)} %bitcast.78), channel_id=1, source_target_pairs={{0,2},{2,4},{4,6},{6,8},{8,10},{10,12},{12,14},{14,16},{16,18},{18... | collective-permute-start | bytes 786440 | tf_op jit(solution)/shard_map/ppermute | solution.py:17
  54.3 5.3 %copy-start = (bf16[8,7,128,128]{3,2,1,0:T(8,128)(2,1)S(1)}, bf16[8,7,128,128]{3,2,1,0:T(8,128)(2,1)}, u32[]{:S(2)}) copy-start(bf16[8,7,128,128]{3,2,1,0:T(8,128)(2,1)} %all-gather.3.cloned.1.call-done) | copy-start | bytes 5505028
  59.5 4.4 %copy-start.4 = (bf16[1024,512]{1,0:T(8,128)(2,1)S(1)}, bf16[1024,512]{1,0:T(8,128)(2,1)}, u32[]{:S(2)}) copy-start(bf16[1024,512]{1,0:T(8,128)(2,1)} %param.5) | copy-start | bytes 3145732
  64.4 8.7 %collective-permute-start.4 = (bf16[256,512]{1,0:T(8,128)(2,1)S(1)}, bf16[256,512]{1,0:T(8,128)(2,1)S(1)}, u32[]{:S(2)}, u32[]{:S(2)}) collective-permute-start(bf16[256,512]{1,0:T(8,128)(2,1)S(1)} %get-tuple-element.7), channel_id=1, source_target_pairs={{0,2},{2,4},{4,6},{6,8},{8,10},{10,12},{12,14},{14,16},{16,18},{18... | collective-permute-start | bytes 786440 | tf_op jit(solution)/shard_map/ppermute | solution.py:17
  66.9 6.1 %collective-permute-start.5 = (bf16[256,512]{1,0:T(8,128)(2,1)S(1)}, bf16[256,512]{1,0:T(8,128)(2,1)S(1)}, u32[]{:S(2)}, u32[]{:S(2)}) collective-permute-start(bf16[256,512]{1,0:T(8,128)(2,1)S(1)} %get-tuple-element.8), channel_id=1, source_target_pairs={{2,0},{4,2},{6,4},{8,6},{10,8},{12,10},{14,12},{16,14},{18,16},{20... | collective-permute-start | bytes 786440 | tf_op jit(solution)/shard_map/ppermute | solution.py:20
  78.4 5.7 %copy-start.2 = (bf16[8,512,128]{1,2,0:T(8,128)(2,1)S(1)}, bf16[8,512,128]{1,2,0:T(8,128)(2,1)}, u32[]{:S(2)}) copy-start(bf16[8,512,128]{1,2,0:T(8,128)(2,1)} %copy-done.1) | copy-start | bytes 3145732
  84.6 8.6 %collective-permute-start.6 = (bf16[256,512]{1,0:T(8,128)(2,1)S(1)}, bf16[256,512]{1,0:T(8,128)(2,1)S(1)}, u32[]{:S(2)}, u32[]{:S(2)}) collective-permute-start(bf16[256,512]{1,0:T(8,128)(2,1)S(1)} %get-tuple-element.5), channel_id=1, source_target_pairs={{0,2},{2,4},{4,6},{6,8},{8,10},{10,12},{12,14},{14,16},{16,18},{18... | collective-permute-start | bytes 786440 | tf_op jit(solution)/shard_map/ppermute | solution.py:17
  87.2 6.1 %collective-permute-start.7 = (bf16[256,512]{1,0:T(8,128)(2,1)S(1)}, bf16[256,512]{1,0:T(8,128)(2,1)S(1)}, u32[]{:S(2)}, u32[]{:S(2)}) collective-permute-start(bf16[256,512]{1,0:T(8,128)(2,1)S(1)} %get-tuple-element.6), channel_id=1, source_target_pairs={{2,0},{4,2},{6,4},{8,6},{10,8},{12,10},{14,12},{16,14},{18,16},{20... | collective-permute-start | bytes 786440 | tf_op jit(solution)/shard_map/ppermute | solution.py:20
  103.9 3.7 %copy-start.5 = (bf16[8,512,128]{1,2,0:T(8,128)(2,1)S(1)}, bf16[8,512,128]{1,2,0:T(8,128)(2,1)}, u32[]{:S(2)}) copy-start(bf16[8,512,128]{1,2,0:T(8,128)(2,1)} %get-tuple-element.13) | copy-start | bytes 3145732
  103.9 12.6 %all-to-all-start = ((bf16[2,512,512]{2,1,0:T(8,128)(2,1)}), bf16[2,512,512]{2,1,0:T(8,128)(2,1)S(1)}, u32[]{:S(2)}, u32[]{:S(2)}) async-start(bf16[2,512,512]{2,1,0:T(8,128)(2,1)} %bitcast.26), calls=%async_computation | async-start | bytes 2097152 | tf_op jit(solution)/shard_map/all_to_all | solution.py:51
  116.5 11.8 %all-to-all-start.1 = ((bf16[2,512,512]{1,2,0:T(8,128)(2,1)}), bf16[2,512,512]{1,2,0:T(8,128)(2,1)S(1)}, u32[]{:S(2)}, u32[]{:S(2)}) async-start(bf16[2,512,512]{1,2,0:T(8,128)(2,1)} %copy.6), calls=%async_computation.1 | async-start | bytes 2097152 | tf_op jit(solution)/shard_map/all_to_all | solution.py:50
  120.1 51.5 %reduce-scatter.2.cloned.1.call-start = ((), (), s32[]{:S(2)}) async-start(), calls=%async_computation.4 | async-start | bytes 3145728 | tf_op jit(solution)/shard_map/reduce_scatter | solution.py:54
  120.5 10.4 %copy-start.6 = (bf16[2,64,8,512]{3,2,0,1:T(8,128)(2,1)}, bf16[2,64,8,512]{3,2,0,1:T(8,128)(2,1)S(1)}, u32[]{:S(2)}) copy-start(bf16[2,64,8,512]{3,2,0,1:T(8,128)(2,1)S(1)} %copy.11) | copy-start | bytes 3145732
  130.9 147.1 %all-gather.5.cloned.1.call-start = ((), (), s32[]{:S(2)}) async-start(), calls=%async_computation.5 | async-start | bytes 3145728 | tf_op jit(solution)/shard_map/all_gather | solution.py:67
Sparse Core Ops, SparseCore 0:
  8.9 32.2 all-gather.2
  131.1 40.4 reduce-scatter.1
  244.1 33.9 all-gather.4
where the time goes:
time: 290 us; the launch traced here: 289 us
  waiting for transfers between devices  128 us (44%)
  blocking collectives  71.1 us (25%)
  matrix products  27.1 us (9%)
  local copies, waits for them, and re-layouts  23.8 us (8%)
  starting transfers between devices  22 us (8%)
  between operations  13.3 us (5%)
  other arithmetic  3.14 us (1%)
    psum x1, blocking collectives, body(): slab_summed = lax.psum(row_block, 'slab')  71.1 us
    reduce_scatter x1, waiting for transfers between devices, body(): lax.psum_scatter(jnp.einsum('rb,rc->bc', columns, strip_applied, preferre...  40.6 us
    all_gather x1, waiting for transfers between devices, body(): lax.all_gather(gram_block, 'band', axis=0, tiled=True)  34.1 us
    gather x4, local copies, waits for them, and re-layouts, apply_local(): picked_blocks = blocks[neighbors]  21 us
    dot_general x4, matrix products, apply_local(): jnp.einsum('rjab,rjbc->rac', full_tiles, picked_blocks, preferred_element...  20.4 us
    all_gather x1, waiting for transfers between devices, body(): full_tiles = lax.all_gather(hamiltonian, 'band', axis=2, tiled=True)  16.2 us
    ppermute x4, waiting for transfers between devices, padded(): lax.ppermute(lax.slice_in_dim(block, block.shape[dim] - width, None, axis...  12 us
    ppermute x4, waiting for transfers between devices, padded(): lax.ppermute(lax.slice_in_dim(block, 0, width, axis=dim), axis, backward)  9.29 us
  transfers between devices with their start and end apart: 13, of which 11 were waited for; matrix products, arithmetic and copies ran while one was open for 3% of the time, Pallas kernels for 0%

commit v1 on v0

--- a/solution.py
+++ b/solution.py
@@ -1,11 +1,17 @@
+import functools
 import math
 
 import jax
 import jax.numpy as jnp
 from jax import lax
+from jax.experimental import pallas as pl
+from jax.experimental.pallas import tpu as pltpu
 from jax.sharding import PartitionSpec as P
 
 FACE = 2
+CHUNKS = 2
+STREAMS = 2
+MESH = pl.DeviceIdType.MESH
 
 
 def padded(block, sides, width):
@@ -33,7 +39,7 @@
     return product.reshape(vector.shape[0], vector.shape[1])
 
 
-def body(hamiltonian, neighbors, orbitals):
+def plain_body(hamiltonian, neighbors, orbitals):
     full_tiles = lax.all_gather(hamiltonian, "band", axis=2, tiled=True)
     first = apply_local(orbitals, full_tiles, neighbors).astype(jnp.bfloat16)
     second = (
@@ -50,27 +56,322 @@
         lax.all_to_all(third, "band", split_axis=0, concat_axis=1, tiled=True),
         lax.all_to_all(applied, "band", split_axis=0, concat_axis=1, tiled=True),
     )
-    columns = strip_third
     row_block = lax.psum_scatter(
-        jnp.einsum("rb,rc->bc", columns, strip_applied, preferred_element_type=jnp.float32).astype(
-            jnp.bfloat16
-        ),
+        jnp.einsum(
+            "rb,rc->bc", strip_third, strip_applied, preferred_element_type=jnp.float32
+        ).astype(jnp.bfloat16),
         "band",
         scatter_dimension=0,
         tiled=True,
     ).astype(jnp.float32)
     slab_summed = lax.psum(row_block, "slab")
     gram_block = (slab_summed * gram_scale).astype(jnp.bfloat16)
-    columns = strip_third
     mixed = jnp.dot(
-        columns,
+        strip_third,
         lax.all_gather(gram_block, "band", axis=0, tiled=True),
         preferred_element_type=jnp.float32,
     )
     return (strip_applied.astype(jnp.float32) - mixed).astype(jnp.bfloat16)
 
 
+def merged_tiles(hamiltonian, neighbors):
+    blocks = hamiltonian.shape[0]
+    within = jnp.arange(blocks, dtype=jnp.int32)
+    layer = FACE + within // FACE * FACE
+    sources = (within, layer, layer + 1, within + 2 * FACE)
+    merged = []
+    for source in sources:
+        total = 0.0
+        for slot in range(hamiltonian.shape[1]):
+            hit = (neighbors[:, slot] == source)[:, None, None]
+            total = total + jnp.where(hit, hamiltonian[:, slot].astype(jnp.float32), 0.0)
+        merged.append(total.astype(jnp.bfloat16))
+    return jnp.concatenate(merged, axis=2)
+
+
+def flipped(index, bit):
+    return index + bit - 2 * bit * lax.rem(lax.div(index, bit), 2)
+
+
+def kernel(
+    slabs, gram_scale, pieces_ref, orbitals_ref, out_ref,
+    tiles, ext0, ext1, ext2, ext3, own_applied, strip3, strip4, gram32, gram16, outgoing, incoming,
+    local_sem, send_sem, recv_sem,
+):
+    slab, band = lax.axis_index("slab"), lax.axis_index("band")
+    other = 1 - band
+    after, before = lax.rem(slab + 1, slabs), lax.rem(slab + slabs - 1, slabs)
+    blocks, part, _ = pieces_ref.shape
+    tile = 2 * part
+    layers = blocks // FACE
+    face = FACE * tile
+    rows = blocks * tile
+    chunks, _, width = ext0.shape
+    strip = rows // 2
+    groups = 2 * chunks
+    ext = [ext0, ext1, ext2, ext3]
+    bits = [1 << i for i in range(slabs.bit_length() - 1)]
+
+    barrier = pltpu.get_barrier_semaphore()
+    greeted = [{"band": other}, {"slab": after}, {"slab": before}]
+    greeted += [{"slab": flipped(slab, bit)} for bit in bits]
+
+    loads = []
+    for c in range(chunks):
+        load = pltpu.make_async_copy(
+            orbitals_ref.at[:, pl.ds(c * width, width)],
+            ext0.at[c, pl.ds(face, rows)],
+            local_sem.at[c],
+        )
+        load.start()
+        loads.append(load)
+    for target in greeted:
+        pl.semaphore_signal(barrier, inc=1, device_id=target, device_id_type=MESH)
+    pl.semaphore_wait(barrier, len(greeted))
+
+    sent = []
+
+    def send(source, target, device):
+        n = len(sent)
+        copy = pltpu.make_async_remote_copy(
+            src_ref=source, dst_ref=target, send_sem=send_sem.at[n], recv_sem=recv_sem.at[n],
+            device_id=device, device_id_type=MESH,
+        )
+        copy.start()
+        sent.append(copy)
+        return copy
+
+    def spans(a):
+        if a == 0:
+            return ((0, 0, tile), (tile, 2 * tile, 3 * tile))
+        return ((0, tile, 3 * tile), (3 * tile, 5 * tile, tile))
+
+    order = [1, 2, 0, 3] if layers == 4 else list(range(layers))
+    tile_copies = {}
+    mine = pl.multiple_of(band * part, part)
+    for layer in order:
+        tile_copies[layer] = []
+        for a in range(FACE):
+            for start, place, size in spans(a):
+                tile_copies[layer].append(send(
+                    pieces_ref.at[layer * FACE + a, :, pl.ds(start, size)],
+                    tiles.at[layer, pl.ds(pl.multiple_of(a * tile + mine, part), part), pl.ds(place, size)],
+                    {"band": other},
+                ))
+
+    def send_halo(k, c, up):
+        if up:
+            return send(ext[k].at[c, pl.ds(rows, face)], ext[k].at[c, pl.ds(0, face)], {"slab": after})
+        return send(
+            ext[k].at[c, pl.ds(face, face)], ext[k].at[c, pl.ds(rows + face, face)], {"slab": before}
+        )
+
+    halos = {}
+    for c in range(chunks):
+        loads[c].wait()
+        halos[0, c] = [send_halo(0, c, False), send_halo(0, c, True)]
+
+    for layer in order:
+        for a in range(FACE):
+            for start, place, size in spans(a):
+                tiles[layer, pl.ds(pl.multiple_of(a * tile + mine, part), part), place:place + size] = (
+                    pieces_ref[layer * FACE + a, :, start:start + size]
+                )
+            hole = (tile, 5 * tile) if a == 0 else (0, 4 * tile)
+            for place in hole:
+                tiles[layer, a * tile:(a + 1) * tile, place:place + tile] = jnp.zeros(
+                    (tile, tile), jnp.bfloat16
+                )
+
+    def apply_layer(k, c, layer):
+        product = jnp.dot(
+            tiles[layer], ext[k][c, layer * face:(layer + 3) * face, :],
+            preferred_element_type=jnp.float32,
+        )
+        inner = slice((layer + 1) * face, (layer + 2) * face)
+        if k == 1 or k == 2:
+            product = 2.0 * product - ext[k - 1][c, inner, :].astype(jnp.float32)
+        if k < 3:
+            ext[k + 1][c, inner, :] = product.astype(jnp.bfloat16)
+        else:
+            own_applied[c, layer * face:(layer + 1) * face, :] = product.astype(jnp.bfloat16)
+
+    strip_copies = {}
+    mine_at = pl.multiple_of(band * strip, strip)
+    theirs_at = pl.multiple_of(other * strip, strip)
+
+    def send_strip(which, c, source, base):
+        place = strip3 if which == 3 else strip4
+        group = band * chunks + c
+        strip_copies[which, c] = send(
+            source.at[c, pl.ds(base + theirs_at, strip)], place.at[group], {"band": other}
+        )
+        place[group] = source[c, pl.ds(base + mine_at, strip), :]
+
+    for k in range(4):
+        for c in range(chunks):
+            inside = list(range(1, layers - 1))
+            for layer in inside:
+                if k == 0 and c == 0:
+                    for copy in tile_copies[layer]:
+                        copy.wait_recv()
+                apply_layer(k, c, layer)
+            for layer, halo in ((0, 1), (layers - 1, 0)):
+                if k == 0 and c == 0:
+                    for copy in tile_copies[layer]:
+                        copy.wait_recv()
+                halos[k, c][halo].wait_recv()
+                apply_layer(k, c, layer)
+                if k < 3:
+                    halos.setdefault((k + 1, c), []).append(send_halo(k + 1, c, layer != 0))
+            if k == 2:
+                send_strip(3, c, ext3, face)
+            if k == 3:
+                send_strip(4, c, own_applied, 0)
+
+    def gram_block(p, q):
+        at = pl.multiple_of((p * groups + q) * width, width)
+        gram32[pl.ds(at, width), :] = lax.dot_general(
+            strip3[p], strip4[q], (((0,), (0,)), ((), ())), preferred_element_type=jnp.float32
+        )
+
+    for c in range(chunks):
+        for d in range(chunks):
+            gram_block(band * chunks + d, band * chunks + c)
+    for c in range(chunks):
+        strip_copies[3, c].wait_recv()
+    for c in range(chunks):
+        for d in range(chunks):
+            gram_block(other * chunks + d, band * chunks + c)
+    for c in range(chunks):
+        strip_copies[4, c].wait_recv()
+        for p in range(groups):
+            gram_block(p, other * chunks + c)
+
+    near, far = bits[0], bits[1:]
+    routes = [
+        [("slab", far[0]), ("band", 1)] + [("slab", b) for b in far[1:]],
+        [("band", 1), ("slab", far[0])] + [("slab", b) for b in far[:0:-1]],
+    ]
+
+    def side_and_target(axis, bit):
+        at = slab if axis == "slab" else band
+        return lax.rem(lax.div(at, bit), 2), {axis: flipped(at, bit)}
+
+    total = gram32.shape[0]
+    used = [0]
+
+    def send_half(from_at, length, target):
+        start = used[0]
+        used[0] += length
+        outgoing[start:start + length, :] = gram32[pl.ds(from_at, length), :].astype(jnp.bfloat16)
+        copy = send(outgoing.at[pl.ds(start, length)], incoming.at[pl.ds(start, length)], target)
+        return copy, start
+
+    def add_half(pending, keep, length):
+        copy, start = pending
+        copy.wait_recv()
+        gram32[pl.ds(keep, length), :] += incoming[start:start + length, :].astype(jnp.float32)
+
+    side, target = side_and_target("slab", near)
+    piece = total // 2 // STREAMS
+    state = []
+    for s in range(STREAMS):
+        there = pl.multiple_of((1 - side) * (total // 2) + s * piece, piece)
+        here = pl.multiple_of(side * (total // 2) + s * piece, piece)
+        state.append([send_half(there, piece, target), here, piece])
+    trail = [[] for _ in range(STREAMS)]
+    for step in range(len(routes[0])):
+        for s in range(STREAMS):
+            pending, here, length = state[s]
+            add_half(pending, here, length)
+            axis, bit = routes[s][step]
+            side, target = side_and_target(axis, bit)
+            half = length // 2
+            trail[s].append((here, length, target))
+            keep = pl.multiple_of(here + side * half, half)
+            away = pl.multiple_of(here + (1 - side) * half, half)
+            state[s] = [send_half(away, half, target), keep, half]
+    side, target = side_and_target("slab", near)
+    back = []
+    for s in range(STREAMS):
+        pending, here, length = state[s]
+        add_half(pending, here, length)
+        gram16[pl.ds(here, length), :] = (gram32[pl.ds(here, length), :] * gram_scale).astype(
+            jnp.bfloat16
+        )
+        back.append([None, here, length])
+    for step in range(len(routes[0]) + 1):
+        for s in range(STREAMS):
+            copy, here, length = back[s]
+            if copy is not None:
+                copy.wait_recv()
+                here, length, _ = trail[s][len(routes[0]) - step]
+            to = trail[s][len(routes[0]) - 1 - step][2] if step < len(routes[0]) else target
+            part_ref = gram16.at[pl.ds(here, length)]
+            back[s] = [send(part_ref, part_ref, to), here, length]
+    for s in range(STREAMS):
+        back[s][0].wait_recv()
+
+    for q in range(groups):
+        mixed = jnp.zeros((strip, width), jnp.float32)
+        for p in range(groups):
+            at = (p * groups + q) * width
+            mixed += jnp.dot(
+                strip3[p], gram16[at:at + width, :], preferred_element_type=jnp.float32
+            )
+        out_ref[:, q * width:(q + 1) * width] = (
+            strip4[q].astype(jnp.float32) - mixed
+        ).astype(jnp.bfloat16)
+    for copy in sent:
+        copy.wait_send()
+
+
+def fused_body(slabs, hamiltonian, neighbors, orbitals):
+    blocks, _, part, tile = hamiltonian.shape
+    rows, bands = orbitals.shape
+    layers = blocks // FACE
+    width = bands // CHUNKS
+    groups = 2 * CHUNKS
+    strip = rows // 2
+    face = FACE * tile
+    total = groups * groups * width
+    gram_scale = 1.0 / math.sqrt(float(rows * slabs) * float(bands * 2))
+    steps = slabs.bit_length()
+    copies = 4 * blocks // 2 + 8 * CHUNKS + 2 * CHUNKS + 2 * STREAMS * steps
+    half = jnp.bfloat16
+    pieces = merged_tiles(hamiltonian, neighbors)
+    flops = 2 * rows * 6 * tile * bands * 4 + 2 * 2 * strip * 4 * bands * bands
+    return pl.pallas_call(
+        functools.partial(kernel, slabs, gram_scale),
+        out_shape=jax.ShapeDtypeStruct((strip, 2 * bands), half),
+        in_specs=[pl.BlockSpec(memory_space=pltpu.VMEM), pl.BlockSpec(memory_space=pl.ANY)],
+        out_specs=pl.BlockSpec(memory_space=pltpu.VMEM),
+        scratch_shapes=[
+            pltpu.VMEM((layers, face, 3 * face), half),
+            *[pltpu.VMEM((CHUNKS, rows + 2 * face, width), half) for _ in range(4)],
+            pltpu.VMEM((CHUNKS, rows, width), half),
+            pltpu.VMEM((groups, strip, width), half),
+            pltpu.VMEM((groups, strip, width), half),
+            pltpu.VMEM((total, width), jnp.float32),
+            pltpu.VMEM((total, width), half),
+            pltpu.VMEM((total, width), half),
+            pltpu.VMEM((total, width), half),
+            pltpu.SemaphoreType.DMA((CHUNKS,)),
+            pltpu.SemaphoreType.DMA((copies,)),
+            pltpu.SemaphoreType.DMA((copies,)),
+        ],
+        compiler_params=pltpu.CompilerParams(
+            collective_id=0, has_side_effects=True, vmem_limit_bytes=48 * 1024 * 1024
+        ),
+        cost_estimate=pl.CostEstimate(flops=flops, bytes_accessed=4 * rows * bands, transcendentals=0),
+    )(pieces, orbitals)
+
+
 def solution(mesh):
     in_specs = (P("slab", None, "band", None), P("slab", None), P("slab", "band"))
     out_specs = P(("slab", "band"), None)
+    slabs, groups = mesh.shape["slab"], mesh.shape["band"]
+    pairs = groups == 2 and slabs >= 8 and slabs & (slabs - 1) == 0
+    body = functools.partial(fused_body, slabs) if pairs else plain_body
     return jax.shard_map(body, mesh=mesh, in_specs=in_specs, out_specs=out_specs, check_vma=False)

time: 290 us -> 100 us (0.34)
  waiting for transfers between devices: 128 us -> 0 us
  Pallas kernels: 0 us -> 94.5 us
  blocking collectives: 71.1 us -> 0 us
  matrix products: 27.1 us -> 0 us
  starting transfers between devices: 22 us -> 0 us
  local copies, waits for them, and re-layouts: 23.8 us -> 3.08 us
  between operations: 13.3 us -> 0.1 us
    pallas_call x0 -> x1, Pallas kernels: none -> 94.5 us  [fused_body(): pl.pallas_call(functools.partial(kernel, slabs, gram_scale), out_shape=ja...]
    psum x1 -> x0, blocking collectives: 71.1 us -> none  [body(): slab_summed = lax.psum(row_block, 'slab')]
    all_gather x2 -> x0, waiting for transfers between devices: 50.3 us -> none  [the longest x1 34.1 us: body(): lax.all_gather(gram_block, 'band', axis=0, tiled=True)]
    reduce_scatter x1 -> x0, waiting for transfers between devices: 40.6 us -> none  [body(): lax.psum_scatter(jnp.einsum('rb,rc->bc', columns, strip_applied, preferre...]
    dot_general x6 -> x0, matrix products: 27.1 us -> none  [the longest x4 20.4 us: apply_local(): jnp.einsum('rjab,rjbc->rac', full_tiles, picked_blocks, preferred_element...]
    ppermute x8 -> x0, waiting for transfers between devices: 21.3 us -> none  [the longest x4 12 us: padded(): lax.ppermute(lax.slice_in_dim(block, block.shape[dim] - width, None, axis...]
    gather x4 -> x0, local copies, waits for them, and re-layouts: 21 us -> none  [apply_local(): picked_blocks = blocks[neighbors]]
    all_to_all x2 -> x0, waiting for transfers between devices: 15.4 us -> none  [the longest x1 7.83 us: body(): lax.all_to_all(third, 'band', split_axis=0, concat_axis=1, tiled=True)]
  transfers between devices with their start and end apart: 13 -> 0, of which waited for: 11 -> 0; matrix products, arithmetic and copies ran while one was open for 3% -> 0% of each run, Pallas kernels for 0% -> 0%
where the time goes in v1:
time: 100 us
  Pallas kernels  94.5 us (94%)
  local copies, waits for them, and re-layouts  3.08 us (3%)
  other arithmetic  2.42 us (2%)
    pallas_call x1, Pallas kernels, fused_body(): pl.pallas_call(functools.partial(kernel, slabs, gram_scale), out_shape=ja...  94.5 us
    convert_element_type x4, other arithmetic, merged_tiles(): merged.append(total.astype(jnp.bfloat16))  2.3 us

profile of v1, /device:TPU:1, one launch (start us, length us, event | category | flops | bytes accessed | tf_op | source)
XLA Modules:
  0.0 100.1 jit_solution(11824131098526085074)
XLA Ops:
  0.0 0.0 copy-start.1
  0.0 1.2 %slice_reduce_fusion.6 = (s32[8]{0:T(128)S(1)}, s32[8]{0:T(128)S(1)}, s32[8]{0:T(128)S(1)}, s32[8]{0:T(128)S(1)}, s32[8]{0:T(128)S(1)}, /*index=5*/s32[8]{0:T(128)S(1)}, s32[8]{0:T(128)S(1)}) fusion(s32[8,7]{1,0:T(8,128)} %param.4), kind=kLoop, calls=%fused_computation.63 | loop fusion | bytes 448 | tf_op jit(solution)/shard_map/slice | solution.py:86
  1.3 1.5 %fusion.6 = bf16[8,64,128]{2,1,0:T(8,128)(2,1)S(1)} fusion(pred[8]{0:T(512)(128)(4,1)S(1)} %get-tuple-element.36, pred[8]{0:T(512)(128)(4,1)S(1)} %get-tuple-element.43, pred[8]{0:T(512)(128)(4,1)S(1)} %get-tuple-element.28, pred[8]{0:T(512)(128)(4,1)S(1)} %get-tuple-element.47, pred[8]{0:T(512)(128)(4,1)S(1)} %get-tuple-element.20, ...), kind=kLoop, calls=%fused_computation.35 | loop fusion | flops 1376256 | bytes 1048632 | tf_op jit(solution)/shard_map/convert_element_type | solution.py:88
  2.8 0.0 copy-done.1
  2.8 0.3 fusion.27
  3.1 0.3 fusion.20
  3.4 0.0 copy-start
  3.4 0.3 fusion.13
  3.7 0.1 pad_maximum_fusion.pieces_ref
  3.7 0.9 copy-done
  4.6 94.5 %shard_map.37 = bf16[512,1024]{1,0:T(8,128)(2,1)S(1)} custom-call(bf16[8,64,512]{2,1,0:T(8,128)(2,1)S(1)} %pad_maximum_fusion.pieces_ref, bf16[1024,512]{1,0:T(8,128)(2,1)S(1)} %copy-done), custom_call_target="tpu_custom_call" | custom-call | flops 5368709120 | bytes 2097152 | tf_op jit(solution)/shard_map/pallas_call | solution.py:345
  99.1 1.0 copy.19
  (4 shorter events, 0.0 us)
Async XLA Ops:
  0.0 2.8 %copy-start.1 = (bf16[8,7,64,128]{3,2,1,0:T(8,128)(2,1)S(1)}, bf16[8,7,64,128]{3,2,1,0:T(8,128)(2,1)}, u32[]{:S(2)}) copy-start(bf16[8,7,64,128]{3,2,1,0:T(8,128)(2,1)} %param.3) | copy-start | bytes 2752516
  3.4 1.2 %copy-start = (bf16[1024,512]{1,0:T(8,128)(2,1)S(1)}, bf16[1024,512]{1,0:T(8,128)(2,1)}, u32[]{:S(2)}) copy-start(bf16[1024,512]{1,0:T(8,128)(2,1)} %orbitals_ref.1) | copy-start | bytes 3145732

commit v2 on v1

--- a/solution.py
+++ b/solution.py
@@ -10,7 +10,6 @@
 
 FACE = 2
 CHUNKS = 2
-STREAMS = 2
 MESH = pl.DeviceIdType.MESH
 
 
@@ -89,14 +88,10 @@
     return jnp.concatenate(merged, axis=2)
 
 
-def flipped(index, bit):
-    return index + bit - 2 * bit * lax.rem(lax.div(index, bit), 2)
-
-
 def kernel(
     slabs, gram_scale, pieces_ref, orbitals_ref, out_ref,
-    tiles, ext0, ext1, ext2, ext3, own_applied, strip3, strip4, gram32, gram16, outgoing, incoming,
-    local_sem, send_sem, recv_sem,
+    tiles, ext0, ext1, ext2, ext3, own_applied, strip3, strip4, own32, to_core, from_core,
+    to_peers, from_peers, gram16, out32, local_sem, send_sem, recv_sem,
 ):
     slab, band = lax.axis_index("slab"), lax.axis_index("band")
     other = 1 - band
@@ -110,11 +105,23 @@
     strip = rows // 2
     groups = 2 * chunks
     ext = [ext0, ext1, ext2, ext3]
-    bits = [1 << i for i in range(slabs.bit_length() - 1)]
+
+    chips, depth = slabs // 2, slabs // 4
+    core, chip = lax.rem(slab, 2), lax.div(slab, 2)
+    column, level = lax.rem(chip, 2), lax.div(chip, 2)
+    sibling = {"slab": chip * 2 + (1 - core)}
+    piece = width // chips
+
+    def at_chip(index, plane):
+        return {"slab": index * 2 + core, "band": plane}
+
+    def ring(offset):
+        return lax.rem(chip + offset, chips)
 
     barrier = pltpu.get_barrier_semaphore()
-    greeted = [{"band": other}, {"slab": after}, {"slab": before}]
-    greeted += [{"slab": flipped(slab, bit)} for bit in bits]
+    greeted = [{"slab": after}, {"slab": before}, sibling]
+    greeted += [at_chip(ring(j), band) for j in range(1, chips)]
+    greeted += [at_chip(ring(j), other) for j in range(chips)]
 
     loads = []
     for c in range(chunks):
@@ -146,7 +153,9 @@
             return ((0, 0, tile), (tile, 2 * tile, 3 * tile))
         return ((0, tile, 3 * tile), (3 * tile, 5 * tile, tile))
 
-    order = [1, 2, 0, 3] if layers == 4 else list(range(layers))
+    outer = [0, layers - 1]
+    inner_layers = list(range(1, layers - 1))
+    order = outer + inner_layers
     tile_copies = {}
     mine = pl.multiple_of(band * part, part)
     for layer in order:
@@ -208,121 +217,196 @@
         )
         place[group] = source[c, pl.ds(base + mine_at, strip), :]
 
-    for k in range(4):
+    def outer_layer(k, c, layer):
+        halos[k, c][1 if layer == 0 else 0].wait_recv()
+        apply_layer(k, c, layer)
+        if k < 3:
+            halos.setdefault((k + 1, c), []).append(send_halo(k + 1, c, layer != 0))
+
+    for layer in outer:
+        for copy in tile_copies[layer]:
+            copy.wait_recv()
         for c in range(chunks):
-            inside = list(range(1, layers - 1))
-            for layer in inside:
-                if k == 0 and c == 0:
-                    for copy in tile_copies[layer]:
-                        copy.wait_recv()
+            outer_layer(0, c, layer)
+    for layer in inner_layers:
+        for copy in tile_copies[layer]:
+            copy.wait_recv()
+        for c in range(chunks):
+            apply_layer(0, c, layer)
+    for k in range(1, 4):
+        for c in range(chunks):
+            for layer in inner_layers:
                 apply_layer(k, c, layer)
-            for layer, halo in ((0, 1), (layers - 1, 0)):
-                if k == 0 and c == 0:
-                    for copy in tile_copies[layer]:
-                        copy.wait_recv()
-                halos[k, c][halo].wait_recv()
-                apply_layer(k, c, layer)
-                if k < 3:
-                    halos.setdefault((k + 1, c), []).append(send_halo(k + 1, c, layer != 0))
+            for layer in outer:
+                outer_layer(k, c, layer)
             if k == 2:
                 send_strip(3, c, ext3, face)
             if k == 3:
                 send_strip(4, c, own_applied, 0)
 
-    def gram_block(p, q):
-        at = pl.multiple_of((p * groups + q) * width, width)
-        gram32[pl.ds(at, width), :] = lax.dot_general(
-            strip3[p], strip4[q], (((0,), (0,)), ((), ())), preferred_element_type=jnp.float32
-        )
-
-    for c in range(chunks):
-        for d in range(chunks):
-            gram_block(band * chunks + d, band * chunks + c)
+    def transposed_dot(left, right):
+        return lax.dot_general(
+            left, right, (((0,), (0,)), ((), ())), preferred_element_type=jnp.float32
+        )
+
+    def unit_start(unit, left, right):
+        to_core[unit] = transposed_dot(left(1 - core), right).astype(jnp.bfloat16)
+        copy = send(to_core.at[unit], from_core.at[unit], sibling)
+        own32[unit] = transposed_dot(left(core), right)
+        return copy
+
+    def unit_spread(unit, copy, place, first, plane):
+        copy.wait_recv()
+        to_peers[unit] = (own32[unit] + from_core[unit].astype(jnp.float32)).astype(jnp.bfloat16)
+        copies = []
+        for j in range(first, chips):
+            target = ring(j)
+            copies.append(send(
+                to_peers.at[unit, pl.ds(pl.multiple_of(target * piece, piece), piece)],
+                from_peers.at[place + j],
+                at_chip(target, plane),
+            ))
+        return copies
+
+    my_piece = pl.multiple_of(chip * piece, piece)
+
+    def summed(unit, places, quad, c):
+        total = to_peers[unit, pl.ds(my_piece, piece), :].astype(jnp.float32)
+        for place in places:
+            total = total + from_peers[place].astype(jnp.float32)
+        row = pl.multiple_of(core * width + my_piece, piece)
+        gram16[quad * chunks + c, pl.ds(row, piece), :] = (total * gram_scale).astype(jnp.bfloat16)
+
+    def pass_on(quad, index, device):
+        row = pl.multiple_of(core * width + index * piece, piece)
+        ref = gram16.at[pl.ds(quad * chunks, chunks), pl.ds(row, piece)]
+        return send(ref, ref, device)
+
+    def place_of(c, kind):
+        return (c * 3 + kind) * chips
+
+    diag = [c for c in range(chunks)]
+    near = [chunks + c for c in range(chunks)]
+    cross = [2 * chunks + c for c in range(chunks)]
+
+    starts = [
+        unit_start(diag[c], lambda d: ext3[d, face:face + rows, :], own_applied[c])
+        for c in range(chunks)
+    ]
+    diag_pieces = [
+        unit_spread(diag[c], starts[c], place_of(c, 0), 1, band) for c in range(chunks)
+    ]
     for c in range(chunks):
         strip_copies[3, c].wait_recv()
+    starts = [
+        unit_start(near[c], lambda d: strip3[other * chunks + d], strip4[band * chunks + c])
+        for c in range(chunks)
+    ]
+    near_pieces = [
+        unit_spread(near[c], starts[c], place_of(c, 1), 1, band) for c in range(chunks)
+    ]
+
+    def level_chip(offset):
+        return lax.rem(level + offset, depth) * 2 + column
+
+    own_diag, other_diag = band * 3, other * 3
     for c in range(chunks):
+        for copy in diag_pieces[c]:
+            copy.wait_recv()
+        summed(diag[c], [place_of(c, 0) + j for j in range(1, chips)], own_diag, c)
+    across = pass_on(own_diag, chip, at_chip(chip, other))
+    beside = level * 2 + (1 - column)
+    side_copies, level_copies = [], []
+
+    def spread_level(quad):
+        side_copies.append(pass_on(quad, chip, at_chip(beside, band)))
+        for j in range(1, depth):
+            level_copies.append((quad, j, pass_on(quad, chip, at_chip(level_chip(j), band))))
+
+    spread_level(own_diag)
+    across.wait_recv()
+    spread_level(other_diag)
+
+    def cross_unit(c):
+        strip_copies[4, c].wait_recv()
+        start = unit_start(cross[c], lambda d: strip3[band * chunks + d], strip4[other * chunks + c])
+        return unit_spread(cross[c], start, place_of(c, 2), 0, other)
+
+    cross_pieces = [cross_unit(0)]
+    for quad, j, copy in level_copies:
+        copy.wait_recv()
+        side_copies.append(pass_on(quad, level_chip(depth - j), at_chip(beside, band)))
+    for c in range(1, chunks):
+        cross_pieces.append(cross_unit(c))
+    for copy in side_copies:
+        copy.wait_recv()
+
+    def send_to_sibling(quad):
+        row = pl.multiple_of(core * width, width)
+        ref = gram16.at[pl.ds(quad * chunks, chunks), pl.ds(row, width)]
+        return send(ref, ref, sibling)
+
+    core_copies = [send_to_sibling(own_diag), send_to_sibling(other_diag)]
+
+    own_off, other_off = other * 2 + band, band * 2 + other
+    for c in range(chunks):
+        for copy in near_pieces[c] + cross_pieces[c]:
+            copy.wait_recv()
+        places = [place_of(c, 1) + j for j in range(1, chips)]
+        places += [place_of(c, 2) + j for j in range(chips)]
+        summed(near[c], places, own_off, c)
+    plane_copies = []
+
+    def spread_plane(index):
+        plane_copies.append((index, [
+            pass_on(own_off, index, at_chip(chip, other)),
+            pass_on(own_off, index, at_chip(beside, band)),
+            pass_on(own_off, index, at_chip(beside, other)),
+        ]))
+
+    level_copies = [
+        (j, pass_on(own_off, chip, at_chip(level_chip(j), band))) for j in range(1, depth)
+    ]
+    spread_plane(chip)
+    core_copies.append(pass_on(own_off, chip, sibling))
+    for j, copy in level_copies:
+        copy.wait_recv()
+        index = level_chip(depth - j)
+        spread_plane(index)
+        core_copies.append(pass_on(own_off, index, sibling))
+    for copy in core_copies[:2]:
+        copy.wait_recv()
+
+    def mix(gr, gc, c):
+        block = gram16[(gr * 2 + gc) * chunks + c]
+        total = jnp.zeros((strip, width), jnp.float32)
         for d in range(chunks):
-            gram_block(other * chunks + d, band * chunks + c)
-    for c in range(chunks):
-        strip_copies[4, c].wait_recv()
-        for p in range(groups):
-            gram_block(p, other * chunks + c)
-
-    near, far = bits[0], bits[1:]
-    routes = [
-        [("slab", far[0]), ("band", 1)] + [("slab", b) for b in far[1:]],
-        [("band", 1), ("slab", far[0])] + [("slab", b) for b in far[:0:-1]],
-    ]
-
-    def side_and_target(axis, bit):
-        at = slab if axis == "slab" else band
-        return lax.rem(lax.div(at, bit), 2), {axis: flipped(at, bit)}
-
-    total = gram32.shape[0]
-    used = [0]
-
-    def send_half(from_at, length, target):
-        start = used[0]
-        used[0] += length
-        outgoing[start:start + length, :] = gram32[pl.ds(from_at, length), :].astype(jnp.bfloat16)
-        copy = send(outgoing.at[pl.ds(start, length)], incoming.at[pl.ds(start, length)], target)
-        return copy, start
-
-    def add_half(pending, keep, length):
-        copy, start = pending
-        copy.wait_recv()
-        gram32[pl.ds(keep, length), :] += incoming[start:start + length, :].astype(jnp.float32)
-
-    side, target = side_and_target("slab", near)
-    piece = total // 2 // STREAMS
-    state = []
-    for s in range(STREAMS):
-        there = pl.multiple_of((1 - side) * (total // 2) + s * piece, piece)
-        here = pl.multiple_of(side * (total // 2) + s * piece, piece)
-        state.append([send_half(there, piece, target), here, piece])
-    trail = [[] for _ in range(STREAMS)]
-    for step in range(len(routes[0])):
-        for s in range(STREAMS):
-            pending, here, length = state[s]
-            add_half(pending, here, length)
-            axis, bit = routes[s][step]
-            side, target = side_and_target(axis, bit)
-            half = length // 2
-            trail[s].append((here, length, target))
-            keep = pl.multiple_of(here + side * half, half)
-            away = pl.multiple_of(here + (1 - side) * half, half)
-            state[s] = [send_half(away, half, target), keep, half]
-    side, target = side_and_target("slab", near)
-    back = []
-    for s in range(STREAMS):
-        pending, here, length = state[s]
-        add_half(pending, here, length)
-        gram16[pl.ds(here, length), :] = (gram32[pl.ds(here, length), :] * gram_scale).astype(
-            jnp.bfloat16
-        )
-        back.append([None, here, length])
-    for step in range(len(routes[0]) + 1):
-        for s in range(STREAMS):
-            copy, here, length = back[s]
-            if copy is not None:
-                copy.wait_recv()
-                here, length, _ = trail[s][len(routes[0]) - step]
-            to = trail[s][len(routes[0]) - 1 - step][2] if step < len(routes[0]) else target
-            part_ref = gram16.at[pl.ds(here, length)]
-            back[s] = [send(part_ref, part_ref, to), here, length]
-    for s in range(STREAMS):
-        back[s][0].wait_recv()
-
-    for q in range(groups):
-        mixed = jnp.zeros((strip, width), jnp.float32)
-        for p in range(groups):
-            at = (p * groups + q) * width
-            mixed += jnp.dot(
-                strip3[p], gram16[at:at + width, :], preferred_element_type=jnp.float32
+            total += jnp.dot(
+                strip3[gr * chunks + d], block[d * width:(d + 1) * width],
+                preferred_element_type=jnp.float32,
             )
-        out_ref[:, q * width:(q + 1) * width] = (
-            strip4[q].astype(jnp.float32) - mixed
-        ).astype(jnp.bfloat16)
+        return total
+
+    for gc in range(2):
+        for c in range(chunks):
+            q = gc * chunks + c
+            out32[q] = strip4[q].astype(jnp.float32) - mix(gc, gc, c)
+    for index, (over, aside, corner) in plane_copies:
+        apart = index + 1 - 2 * column
+        over.wait_recv()
+        core_copies.append(pass_on(other_off, index, sibling))
+        aside.wait_recv()
+        core_copies.append(pass_on(own_off, apart, sibling))
+        corner.wait_recv()
+        core_copies.append(pass_on(other_off, apart, sibling))
+    for copy in core_copies[2:]:
+        copy.wait_recv()
+    for gc in range(2):
+        for c in range(chunks):
+            q = gc * chunks + c
+            out_ref[:, q * width:(q + 1) * width] = (out32[q] - mix(1 - gc, gc, c)).astype(
+                jnp.bfloat16
+            )
     for copy in sent:
         copy.wait_send()
 
@@ -335,10 +419,12 @@
     groups = 2 * CHUNKS
     strip = rows // 2
     face = FACE * tile
-    total = groups * groups * width
+    chips, depth = slabs // 2, slabs // 4
+    piece = width // chips
+    units = 3 * CHUNKS
     gram_scale = 1.0 / math.sqrt(float(rows * slabs) * float(bands * 2))
-    steps = slabs.bit_length()
-    copies = 4 * blocks // 2 + 8 * CHUNKS + 2 * CHUNKS + 2 * STREAMS * steps
+    copies = 2 * blocks + 8 * CHUNKS + 2 * CHUNKS + units * (chips + 1) + 4 * depth + 5
+    copies += 4 * depth + 4 * depth + 4
     half = jnp.bfloat16
     pieces = merged_tiles(hamiltonian, neighbors)
     flops = 2 * rows * 6 * tile * bands * 4 + 2 * 2 * strip * 4 * bands * bands
@@ -353,10 +439,13 @@
             pltpu.VMEM((CHUNKS, rows, width), half),
             pltpu.VMEM((groups, strip, width), half),
             pltpu.VMEM((groups, strip, width), half),
-            pltpu.VMEM((total, width), jnp.float32),
-            pltpu.VMEM((total, width), half),
-            pltpu.VMEM((total, width), half),
-            pltpu.VMEM((total, width), half),
+            pltpu.VMEM((units, width, width), jnp.float32),
+            pltpu.VMEM((units, width, width), half),
+            pltpu.VMEM((units, width, width), half),
+            pltpu.VMEM((units, width, width), half),
+            pltpu.VMEM((units * chips, piece, width), half),
+            pltpu.VMEM((4 * CHUNKS, CHUNKS * width, width), half),
+            pltpu.VMEM((groups, strip, width), jnp.float32),
             pltpu.SemaphoreType.DMA((CHUNKS,)),
             pltpu.SemaphoreType.DMA((copies,)),
             pltpu.SemaphoreType.DMA((copies,)),
@@ -372,6 +461,6 @@
     in_specs = (P("slab", None, "band", None), P("slab", None), P("slab", "band"))
     out_specs = P(("slab", "band"), None)
     slabs, groups = mesh.shape["slab"], mesh.shape["band"]
-    pairs = groups == 2 and slabs >= 8 and slabs & (slabs - 1) == 0
+    pairs = groups == 2 and slabs >= 8 and slabs % 4 == 0 and CHUNKS == 2
     body = functools.partial(fused_body, slabs) if pairs else plain_body
     return jax.shard_map(body, mesh=mesh, in_specs=in_specs, out_specs=out_specs, check_vma=False)

time: 100 us -> 82.8 us (0.83)
  Pallas kernels: 94.5 us -> 77 us
    pallas_call x1, Pallas kernels: 94.5 us -> 77 us  [fused_body(): pl.pallas_call(functools.partial(kernel, slabs, gram_scale), out_shape=ja...]
where the time goes in v2:
time: 82.8 us; the launch traced here: 82.6 us
  Pallas kernels  77 us (93%)
  local copies, waits for them, and re-layouts  3.08 us (4%)
  other arithmetic  2.42 us (3%)
    pallas_call x1, Pallas kernels, fused_body(): pl.pallas_call(functools.partial(kernel, slabs, gram_scale), out_shape=ja...  77 us
    convert_element_type x4, other arithmetic, merged_tiles(): merged.append(total.astype(jnp.bfloat16))  2.3 us
    unnamed x5, local copies, waits for them, and re-layouts  1.85 us

profile of v2, /device:TPU:1, one launch (start us, length us, event | category | flops | bytes accessed | tf_op | source)
XLA Modules:
  0.0 82.6 jit_solution(7401410309852658025)
XLA Ops:
  0.0 0.0 copy-start.1
  0.0 1.2 %slice_reduce_fusion.6 = (s32[8]{0:T(128)S(1)}, s32[8]{0:T(128)S(1)}, s32[8]{0:T(128)S(1)}, s32[8]{0:T(128)S(1)}, s32[8]{0:T(128)S(1)}, /*index=5*/s32[8]{0:T(128)S(1)}, s32[8]{0:T(128)S(1)}) fusion(s32[8,7]{1,0:T(8,128)} %param.4), kind=kLoop, calls=%fused_computation.63 | loop fusion | bytes 448 | tf_op jit(solution)/shard_map/slice | solution.py:85
  1.3 1.5 %fusion.6 = bf16[8,64,128]{2,1,0:T(8,128)(2,1)S(1)} fusion(pred[8]{0:T(512)(128)(4,1)S(1)} %get-tuple-element.36, pred[8]{0:T(512)(128)(4,1)S(1)} %get-tuple-element.43, pred[8]{0:T(512)(128)(4,1)S(1)} %get-tuple-element.28, pred[8]{0:T(512)(128)(4,1)S(1)} %get-tuple-element.47, pred[8]{0:T(512)(128)(4,1)S(1)} %get-tuple-element.20, ...), kind=kLoop, calls=%fused_computation.35 | loop fusion | flops 1376256 | bytes 1048632 | tf_op jit(solution)/shard_map/convert_element_type | solution.py:87
  2.8 0.0 copy-done.1
  2.8 0.3 fusion.27
  3.1 0.3 fusion.20
  3.4 0.0 copy-start
  3.4 0.3 fusion.13
  3.7 0.1 pad_maximum_fusion.pieces_ref
  3.7 0.9 %copy-done = bf16[1024,512]{1,0:T(8,128)(2,1)S(1)} copy-done((bf16[1024,512]{1,0:T(8,128)(2,1)S(1)}, bf16[1024,512]{1,0:T(8,128)(2,1)}, u32[]{:S(2)}) %copy-start) | copy-done | bytes 1048600
  4.6 77.0 %shard_map.37 = bf16[512,1024]{1,0:T(8,128)(2,1)S(1)} custom-call(bf16[8,64,512]{2,1,0:T(8,128)(2,1)S(1)} %pad_maximum_fusion.pieces_ref, bf16[1024,512]{1,0:T(8,128)(2,1)S(1)} %copy-done), custom_call_target="tpu_custom_call" | custom-call | flops 5368709120 | bytes 2097152 | tf_op jit(solution)/shard_map/pallas_call | solution.py:431
  81.6 1.0 %copy.19 = bf16[512,1024]{1,0:T(8,128)(2,1)} copy(bf16[512,1024]{1,0:T(8,128)(2,1)S(1)} %shard_map.37) | data formatting | bytes 2097152
  (4 shorter events, 0.0 us)
Async XLA Ops:
  0.0 2.8 %copy-start.1 = (bf16[8,7,64,128]{3,2,1,0:T(8,128)(2,1)S(1)}, bf16[8,7,64,128]{3,2,1,0:T(8,128)(2,1)}, u32[]{:S(2)}) copy-start(bf16[8,7,64,128]{3,2,1,0:T(8,128)(2,1)} %param.3) | copy-start | bytes 2752516
  3.4 1.2 %copy-start = (bf16[1024,512]{1,0:T(8,128)(2,1)S(1)}, bf16[1024,512]{1,0:T(8,128)(2,1)}, u32[]{:S(2)}) copy-start(bf16[1024,512]{1,0:T(8,128)(2,1)} %orbitals_ref.1) | copy-start | bytes 3145732

commit v3 on v2

--- a/solution.py
+++ b/solution.py
@@ -73,30 +73,15 @@
     return (strip_applied.astype(jnp.float32) - mixed).astype(jnp.bfloat16)
 
 
-def merged_tiles(hamiltonian, neighbors):
-    blocks = hamiltonian.shape[0]
-    within = jnp.arange(blocks, dtype=jnp.int32)
-    layer = FACE + within // FACE * FACE
-    sources = (within, layer, layer + 1, within + 2 * FACE)
-    merged = []
-    for source in sources:
-        total = 0.0
-        for slot in range(hamiltonian.shape[1]):
-            hit = (neighbors[:, slot] == source)[:, None, None]
-            total = total + jnp.where(hit, hamiltonian[:, slot].astype(jnp.float32), 0.0)
-        merged.append(total.astype(jnp.bfloat16))
-    return jnp.concatenate(merged, axis=2)
-
-
 def kernel(
-    slabs, gram_scale, pieces_ref, orbitals_ref, out_ref,
-    tiles, ext0, ext1, ext2, ext3, own_applied, strip3, strip4, own32, to_core, from_core,
+    slabs, gram_scale, neighbors_ref, hamiltonian_ref, orbitals_ref, out_ref,
+    slots, pieces, tiles, ext0, ext1, ext2, ext3, own_applied, strip3, strip4, own32, to_core, from_core,
     to_peers, from_peers, gram16, out32, local_sem, send_sem, recv_sem,
 ):
     slab, band = lax.axis_index("slab"), lax.axis_index("band")
     other = 1 - band
     after, before = lax.rem(slab + 1, slabs), lax.rem(slab + slabs - 1, slabs)
-    blocks, part, _ = pieces_ref.shape
+    blocks, _, part, _ = slots.shape
     tile = 2 * part
     layers = blocks // FACE
     face = FACE * tile
@@ -123,6 +108,16 @@
     greeted += [at_chip(ring(j), band) for j in range(1, chips)]
     greeted += [at_chip(ring(j), other) for j in range(chips)]
 
+    outer = [0, layers - 1]
+    inner_layers = list(range(1, layers - 1))
+    order = outer + inner_layers
+    tile_loads = {}
+    for layer in order:
+        span = pl.ds(layer * FACE, FACE)
+        tile_loads[layer] = pltpu.make_async_copy(
+            hamiltonian_ref.at[span], slots.at[span], local_sem.at[chunks + layer]
+        )
+        tile_loads[layer].start()
     loads = []
     for c in range(chunks):
         load = pltpu.make_async_copy(
@@ -134,63 +129,81 @@
         loads.append(load)
     for target in greeted:
         pl.semaphore_signal(barrier, inc=1, device_id=target, device_id_type=MESH)
-    pl.semaphore_wait(barrier, len(greeted))
-
-    sent = []
-
-    def send(source, target, device):
-        n = len(sent)
-        copy = pltpu.make_async_remote_copy(
-            src_ref=source, dst_ref=target, send_sem=send_sem.at[n], recv_sem=recv_sem.at[n],
-            device_id=device, device_id_type=MESH,
-        )
-        copy.start()
-        sent.append(copy)
-        return copy
 
     def spans(a):
         if a == 0:
             return ((0, 0, tile), (tile, 2 * tile, 3 * tile))
         return ((0, tile, 3 * tile), (3 * tile, 5 * tile, tile))
 
-    outer = [0, layers - 1]
-    inner_layers = list(range(1, layers - 1))
-    order = outer + inner_layers
-    tile_copies = {}
     mine = pl.multiple_of(band * part, part)
-    for layer in order:
-        tile_copies[layer] = []
+
+    def merge(layer):
+        tile_loads[layer].wait()
         for a in range(FACE):
-            for start, place, size in spans(a):
-                tile_copies[layer].append(send(
-                    pieces_ref.at[layer * FACE + a, :, pl.ds(start, size)],
-                    tiles.at[layer, pl.ds(pl.multiple_of(a * tile + mine, part), part), pl.ds(place, size)],
-                    {"band": other},
-                ))
-
-    def send_halo(k, c, up):
-        if up:
-            return send(ext[k].at[c, pl.ds(rows, face)], ext[k].at[c, pl.ds(0, face)], {"slab": after})
-        return send(
-            ext[k].at[c, pl.ds(face, face)], ext[k].at[c, pl.ds(rows + face, face)], {"slab": before}
-        )
-
-    halos = {}
-    for c in range(chunks):
-        loads[c].wait()
-        halos[0, c] = [send_halo(0, c, False), send_halo(0, c, True)]
-
-    for layer in order:
-        for a in range(FACE):
+            row = layer * FACE + a
+            sources = (row, FACE + layer * FACE, FACE + layer * FACE + 1, row + 2 * FACE)
+            totals = [jnp.zeros((part, tile), jnp.float32) for _ in sources]
+            for slot in range(slots.shape[1]):
+                name = neighbors_ref[row, slot]
+                entry = slots[row, slot].astype(jnp.float32)
+                for n, source in enumerate(sources):
+                    totals[n] = totals[n] + jnp.where(name == source, entry, 0.0)
+            merged = jnp.concatenate([total.astype(jnp.bfloat16) for total in totals], axis=1)
+            pieces[row] = merged
             for start, place, size in spans(a):
                 tiles[layer, pl.ds(pl.multiple_of(a * tile + mine, part), part), place:place + size] = (
-                    pieces_ref[layer * FACE + a, :, start:start + size]
+                    merged[:, start:start + size]
                 )
             hole = (tile, 5 * tile) if a == 0 else (0, 4 * tile)
             for place in hole:
                 tiles[layer, a * tile:(a + 1) * tile, place:place + tile] = jnp.zeros(
                     (tile, tile), jnp.bfloat16
                 )
+
+    for layer in outer:
+        merge(layer)
+    pl.semaphore_wait(barrier, len(greeted))
+
+    sent = []
+
+    def send(source, target, device):
+        n = len(sent)
+        copy = pltpu.make_async_remote_copy(
+            src_ref=source, dst_ref=target, send_sem=send_sem.at[n], recv_sem=recv_sem.at[n],
+            device_id=device, device_id_type=MESH,
+        )
+        copy.start()
+        sent.append(copy)
+        return copy
+
+    tile_copies = {}
+
+    def send_tiles(layer):
+        tile_copies[layer] = []
+        for a in range(FACE):
+            for start, place, size in spans(a):
+                tile_copies[layer].append(send(
+                    pieces.at[layer * FACE + a, :, pl.ds(start, size)],
+                    tiles.at[layer, pl.ds(pl.multiple_of(a * tile + mine, part), part), pl.ds(place, size)],
+                    {"band": other},
+                ))
+
+    def send_halo(k, c, up):
+        if up:
+            return send(ext[k].at[c, pl.ds(rows, face)], ext[k].at[c, pl.ds(0, face)], {"slab": after})
+        return send(
+            ext[k].at[c, pl.ds(face, face)], ext[k].at[c, pl.ds(rows + face, face)], {"slab": before}
+        )
+
+    for layer in outer:
+        send_tiles(layer)
+    halos = {}
+    for c in range(chunks):
+        loads[c].wait()
+        halos[0, c] = [send_halo(0, c, False), send_halo(0, c, True)]
+    for layer in inner_layers:
+        merge(layer)
+        send_tiles(layer)
 
     def apply_layer(k, c, layer):
         product = jnp.dot(
@@ -237,6 +250,7 @@
         for c in range(chunks):
             for layer in inner_layers:
                 apply_layer(k, c, layer)
+        for c in range(chunks):
             for layer in outer:
                 outer_layer(k, c, layer)
             if k == 2:
@@ -277,9 +291,9 @@
         row = pl.multiple_of(core * width + my_piece, piece)
         gram16[quad * chunks + c, pl.ds(row, piece), :] = (total * gram_scale).astype(jnp.bfloat16)
 
-    def pass_on(quad, index, device):
+    def pass_on(quad, index, device, span):
         row = pl.multiple_of(core * width + index * piece, piece)
-        ref = gram16.at[pl.ds(quad * chunks, chunks), pl.ds(row, piece)]
+        ref = gram16.at[pl.ds(quad * chunks + span[0], span[1]), pl.ds(row, piece)]
         return send(ref, ref, device)
 
     def place_of(c, kind):
@@ -309,73 +323,94 @@
     def level_chip(offset):
         return lax.rem(level + offset, depth) * 2 + column
 
+    beside = level * 2 + (1 - column)
     own_diag, other_diag = band * 3, other * 3
+    own_off, other_off = other * 2 + band, band * 2 + other
+
+    class Round:
+        def __init__(self, mine, theirs, span):
+            self.mine, self.theirs, self.span = mine, theirs, span
+            self.level_copies, self.side_copies = [], []
+            self.across = pass_on(mine, chip, at_chip(chip, other), span)
+            self.spread(mine)
+
+        def spread(self, quad):
+            self.side_copies.append(pass_on(quad, chip, at_chip(beside, band), self.span))
+            for j in range(1, depth):
+                copy = pass_on(quad, chip, at_chip(level_chip(j), band), self.span)
+                self.level_copies.append((quad, j, copy))
+
+        def second(self):
+            self.across.wait_recv()
+            self.spread(self.theirs)
+
+        def forward(self):
+            for quad, j, copy in self.level_copies:
+                copy.wait_recv()
+                index = level_chip(depth - j)
+                self.side_copies.append(pass_on(quad, index, at_chip(beside, band), self.span))
+
+        def to_sibling(self):
+            for copy in self.side_copies:
+                copy.wait_recv()
+            row = pl.multiple_of(core * width, width)
+            copies = []
+            for quad in (self.mine, self.theirs):
+                ref = gram16.at[pl.ds(quad * chunks + self.span[0], self.span[1]), pl.ds(row, width)]
+                copies.append(send(ref, ref, sibling))
+            return copies
+
+    def cross_unit(c):
+        strip_copies[4, c].wait_recv()
+        start = unit_start(cross[c], lambda d: strip3[band * chunks + d], strip4[other * chunks + c])
+        return unit_spread(cross[c], start, place_of(c, 2), 0, other)
+
+    def sum_off(c, cross_copies):
+        for copy in near_pieces[c] + cross_copies:
+            copy.wait_recv()
+        places = [place_of(c, 1) + j for j in range(1, chips)]
+        places += [place_of(c, 2) + j for j in range(chips)]
+        summed(near[c], places, own_off, c)
+
     for c in range(chunks):
         for copy in diag_pieces[c]:
             copy.wait_recv()
         summed(diag[c], [place_of(c, 0) + j for j in range(1, chips)], own_diag, c)
-    across = pass_on(own_diag, chip, at_chip(chip, other))
-    beside = level * 2 + (1 - column)
-    side_copies, level_copies = [], []
-
-    def spread_level(quad):
-        side_copies.append(pass_on(quad, chip, at_chip(beside, band)))
-        for j in range(1, depth):
-            level_copies.append((quad, j, pass_on(quad, chip, at_chip(level_chip(j), band))))
-
-    spread_level(own_diag)
-    across.wait_recv()
-    spread_level(other_diag)
-
-    def cross_unit(c):
-        strip_copies[4, c].wait_recv()
-        start = unit_start(cross[c], lambda d: strip3[band * chunks + d], strip4[other * chunks + c])
-        return unit_spread(cross[c], start, place_of(c, 2), 0, other)
-
-    cross_pieces = [cross_unit(0)]
-    for quad, j, copy in level_copies:
-        copy.wait_recv()
-        side_copies.append(pass_on(quad, level_chip(depth - j), at_chip(beside, band)))
-    for c in range(1, chunks):
-        cross_pieces.append(cross_unit(c))
-    for copy in side_copies:
-        copy.wait_recv()
-
-    def send_to_sibling(quad):
-        row = pl.multiple_of(core * width, width)
-        ref = gram16.at[pl.ds(quad * chunks, chunks), pl.ds(row, width)]
-        return send(ref, ref, sibling)
-
-    core_copies = [send_to_sibling(own_diag), send_to_sibling(other_diag)]
-
-    own_off, other_off = other * 2 + band, band * 2 + other
-    for c in range(chunks):
-        for copy in near_pieces[c] + cross_pieces[c]:
-            copy.wait_recv()
-        places = [place_of(c, 1) + j for j in range(1, chips)]
-        places += [place_of(c, 2) + j for j in range(chips)]
-        summed(near[c], places, own_off, c)
-    plane_copies = []
+    rounds = [Round(own_diag, other_diag, (0, chunks))]
+    rounds[0].second()
+    cross_copies = cross_unit(0)
+    rounds[0].forward()
+    last = chunks - 1
+    for c in range(last):
+        sum_off(c, cross_copies)
+        rounds.append(Round(own_off, other_off, (c, 1)))
+        cross_copies = cross_unit(c + 1)
+        rounds[-1].second()
+    early_copies = rounds[0].to_sibling()
+    for turn in rounds[1:]:
+        turn.forward()
+
+    sum_off(last, cross_copies)
+    span = (last, 1)
+    plane_copies, core_copies = [], []
 
     def spread_plane(index):
         plane_copies.append((index, [
-            pass_on(own_off, index, at_chip(chip, other)),
-            pass_on(own_off, index, at_chip(beside, band)),
-            pass_on(own_off, index, at_chip(beside, other)),
+            pass_on(own_off, index, at_chip(chip, other), span),
+            pass_on(own_off, index, at_chip(beside, band), span),
+            pass_on(own_off, index, at_chip(beside, other), span),
         ]))
+        core_copies.append(pass_on(own_off, index, sibling, span))
 
     level_copies = [
-        (j, pass_on(own_off, chip, at_chip(level_chip(j), band))) for j in range(1, depth)
+        (j, pass_on(own_off, chip, at_chip(level_chip(j), band), span)) for j in range(1, depth)
     ]
     spread_plane(chip)
-    core_copies.append(pass_on(own_off, chip, sibling))
     for j, copy in level_copies:
         copy.wait_recv()
-        index = level_chip(depth - j)
-        spread_plane(index)
-        core_copies.append(pass_on(own_off, index, sibling))
-    for copy in core_copies[:2]:
-        copy.wait_recv()
+        spread_plane(level_chip(depth - j))
+    for turn in rounds[1:]:
+        early_copies += turn.to_sibling()
 
     def mix(gr, gc, c):
         block = gram16[(gr * 2 + gc) * chunks + c]
@@ -387,32 +422,40 @@
             )
         return total
 
+    def finish(gc, c):
+        q = gc * chunks + c
+        out_ref[:, q * width:(q + 1) * width] = (out32[gc] - mix(1 - gc, gc, c)).astype(jnp.bfloat16)
+
+    def begin(gc, c):
+        out32[gc] = strip4[gc * chunks + c].astype(jnp.float32) - mix(gc, gc, c)
+
+    for copy in early_copies:
+        copy.wait_recv()
+    for c in range(last):
+        for gc in range(2):
+            begin(gc, c)
+            finish(gc, c)
     for gc in range(2):
-        for c in range(chunks):
-            q = gc * chunks + c
-            out32[q] = strip4[q].astype(jnp.float32) - mix(gc, gc, c)
+        begin(gc, last)
     for index, (over, aside, corner) in plane_copies:
         apart = index + 1 - 2 * column
         over.wait_recv()
-        core_copies.append(pass_on(other_off, index, sibling))
+        core_copies.append(pass_on(other_off, index, sibling, span))
         aside.wait_recv()
-        core_copies.append(pass_on(own_off, apart, sibling))
+        core_copies.append(pass_on(own_off, apart, sibling, span))
         corner.wait_recv()
-        core_copies.append(pass_on(other_off, apart, sibling))
-    for copy in core_copies[2:]:
+        core_copies.append(pass_on(other_off, apart, sibling, span))
+    for copy in core_copies:
         copy.wait_recv()
     for gc in range(2):
-        for c in range(chunks):
-            q = gc * chunks + c
-            out_ref[:, q * width:(q + 1) * width] = (out32[q] - mix(1 - gc, gc, c)).astype(
-                jnp.bfloat16
-            )
+        finish(gc, last)
+    assert len(sent) <= send_sem.shape[0]
     for copy in sent:
         copy.wait_send()
 
 
 def fused_body(slabs, hamiltonian, neighbors, orbitals):
-    blocks, _, part, tile = hamiltonian.shape
+    blocks, slots, part, tile = hamiltonian.shape
     rows, bands = orbitals.shape
     layers = blocks // FACE
     width = bands // CHUNKS
@@ -424,16 +467,21 @@
     units = 3 * CHUNKS
     gram_scale = 1.0 / math.sqrt(float(rows * slabs) * float(bands * 2))
     copies = 2 * blocks + 8 * CHUNKS + 2 * CHUNKS + units * (chips + 1) + 4 * depth + 5
-    copies += 4 * depth + 4 * depth + 4
+    copies += (CHUNKS - 1) * (4 * depth + 3) + 8 * depth
     half = jnp.bfloat16
-    pieces = merged_tiles(hamiltonian, neighbors)
     flops = 2 * rows * 6 * tile * bands * 4 + 2 * 2 * strip * 4 * bands * bands
     return pl.pallas_call(
         functools.partial(kernel, slabs, gram_scale),
         out_shape=jax.ShapeDtypeStruct((strip, 2 * bands), half),
-        in_specs=[pl.BlockSpec(memory_space=pltpu.VMEM), pl.BlockSpec(memory_space=pl.ANY)],
+        in_specs=[
+            pl.BlockSpec(memory_space=pltpu.SMEM),
+            pl.BlockSpec(memory_space=pl.ANY),
+            pl.BlockSpec(memory_space=pl.ANY),
+        ],
         out_specs=pl.BlockSpec(memory_space=pltpu.VMEM),
         scratch_shapes=[
+            pltpu.VMEM((blocks, slots, part, tile), half),
+            pltpu.VMEM((blocks, part, 4 * tile), half),
             pltpu.VMEM((layers, face, 3 * face), half),
             *[pltpu.VMEM((CHUNKS, rows + 2 * face, width), half) for _ in range(4)],
             pltpu.VMEM((CHUNKS, rows, width), half),
@@ -445,8 +493,8 @@
             pltpu.VMEM((units, width, width), half),
             pltpu.VMEM((units * chips, piece, width), half),
             pltpu.VMEM((4 * CHUNKS, CHUNKS * width, width), half),
-            pltpu.VMEM((groups, strip, width), jnp.float32),
-            pltpu.SemaphoreType.DMA((CHUNKS,)),
+            pltpu.VMEM((2, strip, width), jnp.float32),
+            pltpu.SemaphoreType.DMA((CHUNKS + layers,)),
             pltpu.SemaphoreType.DMA((copies,)),
             pltpu.SemaphoreType.DMA((copies,)),
         ],
@@ -454,7 +502,7 @@
             collective_id=0, has_side_effects=True, vmem_limit_bytes=48 * 1024 * 1024
         ),
         cost_estimate=pl.CostEstimate(flops=flops, bytes_accessed=4 * rows * bands, transcendentals=0),
-    )(pieces, orbitals)
+    )(neighbors, hamiltonian, orbitals)
 
 
 def solution(mesh):

time: 82.8 us -> 85.3 us (1.030)
  Pallas kernels: 77 us -> 81 us
  other arithmetic: 2.42 us -> 0 us
  local copies, waits for them, and re-layouts: 3.08 us -> 4.06 us
    pallas_call x1, Pallas kernels: 77 us -> 81 us  [fused_body(): pl.pallas_call(functools.partial(kernel, slabs, gram_scale), out_shape=ja...]
    convert_element_type x4 -> x0, other arithmetic: 2.3 us -> none  [merged_tiles(): merged.append(total.astype(jnp.bfloat16))]
    unnamed x5 -> x7, local copies, waits for them, and re-layouts: 1.85 us -> 4.06 us
    slice x1 -> x0, local copies, waits for them, and re-layouts: 1.23 us -> none  [merged_tiles(): hit = (neighbors[:, slot] == source)[:, None, None]]
where the time goes in v3:
time: 85.3 us; the launch traced here: 85.1 us
  Pallas kernels  81 us (95%)
  local copies, waits for them, and re-layouts  4.06 us (5%)
    pallas_call x1, Pallas kernels, fused_body(): pl.pallas_call(functools.partial(kernel, slabs, gram_scale), out_shape=ja...  81 us
    unnamed x7, local copies, waits for them, and re-layouts  4.06 us

profile of v3, /device:TPU:1, one launch (start us, length us, event | category | flops | bytes accessed | tf_op | source)
XLA Modules:
  0.0 85.1 jit_solution(15049507402999472244)
XLA Ops:
  0.0 0.0 copy-start
  0.0 1.2 %copy-done = bf16[1024,512]{1,0:T(8,128)(2,1)S(1)} copy-done((bf16[1024,512]{1,0:T(8,128)(2,1)S(1)}, bf16[1024,512]{1,0:T(8,128)(2,1)}, u32[]{:S(2)}) %copy-start) | copy-done | bytes 1048600
  1.2 0.0 copy-start.1
  1.2 1.2 %copy-done.1 = bf16[8,7,64,128]{3,2,1,0:T(8,128)(2,1)S(1)} copy-done((bf16[8,7,64,128]{3,2,1,0:T(8,128)(2,1)S(1)}, bf16[8,7,64,128]{3,2,1,0:T(8,128)(2,1)}, u32[]{:S(2)}) %copy-start.1) | copy-done | bytes 917528
  2.4 0.0 copy-start.2
  2.4 0.7 copy-done.2
  3.1 81.0 %shard_map.37 = bf16[512,1024]{1,0:T(8,128)(2,1)S(1)} custom-call(s32[8,7]{1,0:T(8,128)S(1)} %copy-done.2, bf16[8,7,64,128]{3,2,1,0:T(8,128)(2,1)S(1)} %copy-done.1, bf16[1024,512]{1,0:T(8,128)(2,1)S(1)} %copy-done), custom_call_target="tpu_custom_call" | custom-call | flops 5368709120 | bytes 2097152 | tf_op jit(solution)/shard_map/pallas_call | solution.py:473
  84.1 1.0 %copy.5 = bf16[512,1024]{1,0:T(8,128)(2,1)} copy(bf16[512,1024]{1,0:T(8,128)(2,1)S(1)} %shard_map.37) | data formatting | bytes 2097152
Async XLA Ops:
  0.0 1.2 %copy-start = (bf16[1024,512]{1,0:T(8,128)(2,1)S(1)}, bf16[1024,512]{1,0:T(8,128)(2,1)}, u32[]{:S(2)}) copy-start(bf16[1024,512]{1,0:T(8,128)(2,1)} %orbitals_ref.1) | copy-start | bytes 3145732
  1.2 1.2 %copy-start.1 = (bf16[8,7,64,128]{3,2,1,0:T(8,128)(2,1)S(1)}, bf16[8,7,64,128]{3,2,1,0:T(8,128)(2,1)}, u32[]{:S(2)}) copy-start(bf16[8,7,64,128]{3,2,1,0:T(8,128)(2,1)} %hamiltonian_ref.1) | copy-start | bytes 2752516
  2.4 0.7 copy-start.2

commit v4 on v3

--- a/solution.py
+++ b/solution.py
@@ -75,8 +75,8 @@
 
 def kernel(
     slabs, gram_scale, neighbors_ref, hamiltonian_ref, orbitals_ref, out_ref,
-    slots, pieces, tiles, ext0, ext1, ext2, ext3, own_applied, strip3, strip4, own32, to_core, from_core,
-    to_peers, from_peers, gram16, out32, local_sem, send_sem, recv_sem,
+    names, slots, pieces, tiles, ext0, ext1, ext2, ext3, own_applied, strip3, strip4, own32, to_core, from_core,
+    to_peers, from_peers, crossing, gram16, out32, local_sem, send_sem, recv_sem,
 ):
     slab, band = lax.axis_index("slab"), lax.axis_index("band")
     other = 1 - band
@@ -111,6 +111,8 @@
     outer = [0, layers - 1]
     inner_layers = list(range(1, layers - 1))
     order = outer + inner_layers
+    name_load = pltpu.make_async_copy(neighbors_ref, names, local_sem.at[chunks + layers])
+    name_load.start()
     tile_loads = {}
     for layer in order:
         span = pl.ds(layer * FACE, FACE)
@@ -144,7 +146,7 @@
             sources = (row, FACE + layer * FACE, FACE + layer * FACE + 1, row + 2 * FACE)
             totals = [jnp.zeros((part, tile), jnp.float32) for _ in sources]
             for slot in range(slots.shape[1]):
-                name = neighbors_ref[row, slot]
+                name = names[row, slot]
                 entry = slots[row, slot].astype(jnp.float32)
                 for n, source in enumerate(sources):
                     totals[n] = totals[n] + jnp.where(name == source, entry, 0.0)
@@ -160,6 +162,7 @@
                     (tile, tile), jnp.bfloat16
                 )
 
+    name_load.wait()
     for layer in outer:
         merge(layer)
     pl.semaphore_wait(barrier, len(greeted))
@@ -228,7 +231,10 @@
         strip_copies[which, c] = send(
             source.at[c, pl.ds(base + theirs_at, strip)], place.at[group], {"band": other}
         )
-        place[group] = source[c, pl.ds(base + mine_at, strip), :]
+
+    def keep_strip(which, c, source, base):
+        place = strip3 if which == 3 else strip4
+        place[band * chunks + c] = source[c, pl.ds(base + mine_at, strip), :]
 
     def outer_layer(k, c, layer):
         halos[k, c][1 if layer == 0 else 0].wait_recv()
@@ -255,8 +261,11 @@
                 outer_layer(k, c, layer)
             if k == 2:
                 send_strip(3, c, ext3, face)
+                keep_strip(3, c, ext3, face)
             if k == 3:
-                send_strip(4, c, own_applied, 0)
+                if c < chunks - 1:
+                    send_strip(4, c, own_applied, 0)
+                keep_strip(4, c, own_applied, 0)
 
     def transposed_dot(left, right):
         return lax.dot_general(
@@ -284,10 +293,14 @@
 
     my_piece = pl.multiple_of(chip * piece, piece)
 
-    def summed(unit, places, quad, c):
+    def piece_sum(unit, places):
         total = to_peers[unit, pl.ds(my_piece, piece), :].astype(jnp.float32)
         for place in places:
             total = total + from_peers[place].astype(jnp.float32)
+        return total
+
+    def summed(unit, places, quad, c):
+        total = piece_sum(unit, places)
         row = pl.multiple_of(core * width + my_piece, piece)
         gram16[quad * chunks + c, pl.ds(row, piece), :] = (total * gram_scale).astype(jnp.bfloat16)
 
@@ -299,6 +312,7 @@
     def place_of(c, kind):
         return (c * 3 + kind) * chips
 
+    last = chunks - 1
     diag = [c for c in range(chunks)]
     near = [chunks + c for c in range(chunks)]
     cross = [2 * chunks + c for c in range(chunks)]
@@ -327,90 +341,76 @@
     own_diag, other_diag = band * 3, other * 3
     own_off, other_off = other * 2 + band, band * 2 + other
 
-    class Round:
-        def __init__(self, mine, theirs, span):
-            self.mine, self.theirs, self.span = mine, theirs, span
-            self.level_copies, self.side_copies = [], []
-            self.across = pass_on(mine, chip, at_chip(chip, other), span)
-            self.spread(mine)
-
-        def spread(self, quad):
-            self.side_copies.append(pass_on(quad, chip, at_chip(beside, band), self.span))
-            for j in range(1, depth):
-                copy = pass_on(quad, chip, at_chip(level_chip(j), band), self.span)
-                self.level_copies.append((quad, j, copy))
-
-        def second(self):
-            self.across.wait_recv()
-            self.spread(self.theirs)
-
-        def forward(self):
-            for quad, j, copy in self.level_copies:
-                copy.wait_recv()
-                index = level_chip(depth - j)
-                self.side_copies.append(pass_on(quad, index, at_chip(beside, band), self.span))
-
-        def to_sibling(self):
-            for copy in self.side_copies:
-                copy.wait_recv()
-            row = pl.multiple_of(core * width, width)
-            copies = []
-            for quad in (self.mine, self.theirs):
-                ref = gram16.at[pl.ds(quad * chunks + self.span[0], self.span[1]), pl.ds(row, width)]
-                copies.append(send(ref, ref, sibling))
-            return copies
-
-    def cross_unit(c):
+    for c in range(chunks):
+        for copy in diag_pieces[c]:
+            copy.wait_recv()
+        summed(diag[c], [place_of(c, 0) + j for j in range(1, chips)], own_diag, c)
+
+    whole = (0, chunks)
+    across = pass_on(own_diag, chip, at_chip(chip, other), whole)
+    send_strip(4, last, own_applied, 0)
+    diag_levels, diag_sides = [], []
+
+    def spread_diag(quad):
+        diag_sides.append(pass_on(quad, chip, at_chip(beside, band), whole))
+        for j in range(1, depth):
+            diag_levels.append((quad, j, pass_on(quad, chip, at_chip(level_chip(j), band), whole)))
+
+    def block_to_sibling(quad, span):
+        row = pl.multiple_of(core * width, width)
+        ref = gram16.at[pl.ds(quad * chunks + span[0], span[1]), pl.ds(row, width)]
+        return send(ref, ref, sibling)
+
+    spread_diag(own_diag)
+
+    def cross_unit(c, first, plane):
         strip_copies[4, c].wait_recv()
         start = unit_start(cross[c], lambda d: strip3[band * chunks + d], strip4[other * chunks + c])
-        return unit_spread(cross[c], start, place_of(c, 2), 0, other)
-
-    def sum_off(c, cross_copies):
-        for copy in near_pieces[c] + cross_copies:
+        return unit_spread(cross[c], start, place_of(c, 2), first, plane)
+
+    cross_copies = {c: cross_unit(c, 1, band) for c in range(last)}
+    across.wait_recv()
+    spread_diag(other_diag)
+    for c in range(last):
+        for copy in cross_copies[c]:
+            copy.wait_recv()
+        total = piece_sum(cross[c], [place_of(c, 2) + j for j in range(1, chips)])
+        crossing[c] = total.astype(jnp.bfloat16)
+        cross_copies[c] = [send(crossing.at[c], from_peers.at[place_of(c, 2)], at_chip(chip, other))]
+    for quad, j, copy in diag_levels:
+        copy.wait_recv()
+        diag_sides.append(pass_on(quad, level_chip(depth - j), at_chip(beside, band), whole))
+    cross_copies[last] = cross_unit(last, 0, other)
+    for copy in diag_sides:
+        copy.wait_recv()
+    early_copies = [block_to_sibling(quad, whole) for quad in (own_diag, other_diag)]
+
+    def sum_off(c):
+        for copy in near_pieces[c] + cross_copies[c]:
             copy.wait_recv()
         places = [place_of(c, 1) + j for j in range(1, chips)]
-        places += [place_of(c, 2) + j for j in range(chips)]
+        places += [place_of(c, 2) + j for j in range(chips if c == last else 1)]
         summed(near[c], places, own_off, c)
 
-    for c in range(chunks):
-        for copy in diag_pieces[c]:
-            copy.wait_recv()
-        summed(diag[c], [place_of(c, 0) + j for j in range(1, chips)], own_diag, c)
-    rounds = [Round(own_diag, other_diag, (0, chunks))]
-    rounds[0].second()
-    cross_copies = cross_unit(0)
-    rounds[0].forward()
-    last = chunks - 1
-    for c in range(last):
-        sum_off(c, cross_copies)
-        rounds.append(Round(own_off, other_off, (c, 1)))
-        cross_copies = cross_unit(c + 1)
-        rounds[-1].second()
-    early_copies = rounds[0].to_sibling()
-    for turn in rounds[1:]:
-        turn.forward()
-
-    sum_off(last, cross_copies)
-    span = (last, 1)
-    plane_copies, core_copies = [], []
-
-    def spread_plane(index):
-        plane_copies.append((index, [
+    def spread_plane(index, span):
+        return [
             pass_on(own_off, index, at_chip(chip, other), span),
             pass_on(own_off, index, at_chip(beside, band), span),
             pass_on(own_off, index, at_chip(beside, other), span),
-        ]))
-        core_copies.append(pass_on(own_off, index, sibling, span))
-
-    level_copies = [
-        (j, pass_on(own_off, chip, at_chip(level_chip(j), band), span)) for j in range(1, depth)
-    ]
-    spread_plane(chip)
-    for j, copy in level_copies:
-        copy.wait_recv()
-        spread_plane(level_chip(depth - j))
-    for turn in rounds[1:]:
-        early_copies += turn.to_sibling()
+        ]
+
+    plane_copies = {}
+    for c in range(chunks):
+        sum_off(c)
+        span = (c, 1)
+        level_copies = [
+            (j, pass_on(own_off, chip, at_chip(level_chip(j), band), span))
+            for j in range(1, depth)
+        ]
+        plane_copies[c] = spread_plane(chip, span)
+        for j, copy in level_copies:
+            copy.wait_recv()
+            plane_copies[c] += spread_plane(level_chip(depth - j), span)
 
     def mix(gr, gc, c):
         block = gram16[(gr * 2 + gc) * chunks + c]
@@ -422,33 +422,25 @@
             )
         return total
 
-    def finish(gc, c):
-        q = gc * chunks + c
-        out_ref[:, q * width:(q + 1) * width] = (out32[gc] - mix(1 - gc, gc, c)).astype(jnp.bfloat16)
-
-    def begin(gc, c):
-        out32[gc] = strip4[gc * chunks + c].astype(jnp.float32) - mix(gc, gc, c)
-
     for copy in early_copies:
         copy.wait_recv()
-    for c in range(last):
+    for gc in range(2):
+        for c in range(chunks):
+            q = gc * chunks + c
+            out32[q] = strip4[q].astype(jnp.float32) - mix(gc, gc, c)
+    core_copies = {}
+    for c in range(chunks):
+        for copy in plane_copies[c]:
+            copy.wait_recv()
+        core_copies[c] = [block_to_sibling(quad, (c, 1)) for quad in (own_off, other_off)]
+    for c in range(chunks):
+        for copy in core_copies[c]:
+            copy.wait_recv()
         for gc in range(2):
-            begin(gc, c)
-            finish(gc, c)
-    for gc in range(2):
-        begin(gc, last)
-    for index, (over, aside, corner) in plane_copies:
-        apart = index + 1 - 2 * column
-        over.wait_recv()
-        core_copies.append(pass_on(other_off, index, sibling, span))
-        aside.wait_recv()
-        core_copies.append(pass_on(own_off, apart, sibling, span))
-        corner.wait_recv()
-        core_copies.append(pass_on(other_off, apart, sibling, span))
-    for copy in core_copies:
-        copy.wait_recv()
-    for gc in range(2):
-        finish(gc, last)
+            q = gc * chunks + c
+            out_ref[:, q * width:(q + 1) * width] = (out32[q] - mix(1 - gc, gc, c)).astype(
+                jnp.bfloat16
+            )
     assert len(sent) <= send_sem.shape[0]
     for copy in sent:
         copy.wait_send()
@@ -467,19 +459,20 @@
     units = 3 * CHUNKS
     gram_scale = 1.0 / math.sqrt(float(rows * slabs) * float(bands * 2))
     copies = 2 * blocks + 8 * CHUNKS + 2 * CHUNKS + units * (chips + 1) + 4 * depth + 5
-    copies += (CHUNKS - 1) * (4 * depth + 3) + 8 * depth
+    copies += CHUNKS * (4 * depth + 4)
     half = jnp.bfloat16
     flops = 2 * rows * 6 * tile * bands * 4 + 2 * 2 * strip * 4 * bands * bands
     return pl.pallas_call(
         functools.partial(kernel, slabs, gram_scale),
         out_shape=jax.ShapeDtypeStruct((strip, 2 * bands), half),
         in_specs=[
-            pl.BlockSpec(memory_space=pltpu.SMEM),
-            pl.BlockSpec(memory_space=pl.ANY),
-            pl.BlockSpec(memory_space=pl.ANY),
+            pl.BlockSpec(memory_space=pltpu.HBM),
+            pl.BlockSpec(memory_space=pltpu.HBM),
+            pl.BlockSpec(memory_space=pltpu.HBM),
         ],
         out_specs=pl.BlockSpec(memory_space=pltpu.VMEM),
         scratch_shapes=[
+            pltpu.SMEM((blocks, slots), jnp.int32),
             pltpu.VMEM((blocks, slots, part, tile), half),
             pltpu.VMEM((blocks, part, 4 * tile), half),
             pltpu.VMEM((layers, face, 3 * face), half),
@@ -492,14 +485,15 @@
             pltpu.VMEM((units, width, width), half),
             pltpu.VMEM((units, width, width), half),
             pltpu.VMEM((units * chips, piece, width), half),
+            pltpu.VMEM((CHUNKS, piece, width), half),
             pltpu.VMEM((4 * CHUNKS, CHUNKS * width, width), half),
-            pltpu.VMEM((2, strip, width), jnp.float32),
-            pltpu.SemaphoreType.DMA((CHUNKS + layers,)),
+            pltpu.VMEM((groups, strip, width), jnp.float32),
+            pltpu.SemaphoreType.DMA((CHUNKS + layers + 1,)),
             pltpu.SemaphoreType.DMA((copies,)),
             pltpu.SemaphoreType.DMA((copies,)),
         ],
         compiler_params=pltpu.CompilerParams(
-            collective_id=0, has_side_effects=True, vmem_limit_bytes=48 * 1024 * 1024
+            collective_id=0, has_side_effects=True, vmem_limit_bytes=63 * 1024 * 1024 + 512 * 1024
         ),
         cost_estimate=pl.CostEstimate(flops=flops, bytes_accessed=4 * rows * bands, transcendentals=0),
     )(neighbors, hamiltonian, orbitals)

time: 85.3 us -> 83 us (0.973)
  local copies, waits for them, and re-layouts: 4.06 us -> 2.26 us
    unnamed x7 -> x1, local copies, waits for them, and re-layouts: 4.06 us -> 2.26 us
where the time goes in v4:
time: 83 us; the launch traced here: 82.8 us
  Pallas kernels  80.5 us (97%)
  local copies, waits for them, and re-layouts  2.26 us (3%)
    pallas_call x1, Pallas kernels, fused_body(): pl.pallas_call(functools.partial(kernel, slabs, gram_scale), out_shape=ja...  80.5 us
    unnamed x1, local copies, waits for them, and re-layouts  2.26 us

profile of v4, /device:TPU:1, one launch (start us, length us, event | category | flops | bytes accessed | tf_op | source)
XLA Modules:
  0.0 82.8 jit_solution(7301119848879534795)
XLA Ops:
  0.0 80.5 %shard_map.37 = bf16[512,1024]{1,0:T(8,128)(2,1)} custom-call(s32[8,7]{1,0:T(8,128)} %neighbors_ref.1, bf16[8,7,64,128]{3,2,1,0:T(8,128)(2,1)} %hamiltonian_ref.1, bf16[1024,512]{1,0:T(8,128)(2,1)} %orbitals_ref.1), custom_call_target="tpu_custom_call" | custom-call | flops 5368709120 | bytes 2097152 | tf_op jit(solution)/shard_map/pallas_call | solution.py:465
  80.5 2.3 %copy.5 = bf16[512,1024]{1,0:T(8,128)(2,1)} copy(bf16[512,1024]{1,0:T(8,128)(2,1)} %shard_map.37) | data formatting | bytes 2097152

commit v5 on v4

--- a/solution.py
+++ b/solution.py
@@ -75,7 +75,7 @@
 
 def kernel(
     slabs, gram_scale, neighbors_ref, hamiltonian_ref, orbitals_ref, out_ref,
-    names, slots, pieces, tiles, ext0, ext1, ext2, ext3, own_applied, strip3, strip4, own32, to_core, from_core,
+    names, slots, pieces, arrived, tiles, slab_t, other_t, ext0, ext1, ext2, ext3, own_applied, strip3, strip4, own32, to_core, from_core,
     to_peers, from_peers, crossing, gram16, out32, local_sem, send_sem, recv_sem,
 ):
     slab, band = lax.axis_index("slab"), lax.axis_index("band")
@@ -137,7 +137,10 @@
             return ((0, 0, tile), (tile, 2 * tile, 3 * tile))
         return ((0, tile, 3 * tile), (3 * tile, 5 * tile, tile))
 
-    mine = pl.multiple_of(band * part, part)
+    def put(layer, a, side, merged):
+        row = pl.multiple_of(a * tile + side * part, part)
+        for start, place, size in spans(a):
+            tiles[layer, pl.ds(row, part), place:place + size] = merged[:, start:start + size]
 
     def merge(layer):
         tile_loads[layer].wait()
@@ -151,11 +154,8 @@
                 for n, source in enumerate(sources):
                     totals[n] = totals[n] + jnp.where(name == source, entry, 0.0)
             merged = jnp.concatenate([total.astype(jnp.bfloat16) for total in totals], axis=1)
-            pieces[row] = merged
-            for start, place, size in spans(a):
-                tiles[layer, pl.ds(pl.multiple_of(a * tile + mine, part), part), place:place + size] = (
-                    merged[:, start:start + size]
-                )
+            pieces[layer, a] = merged
+            put(layer, a, band, merged)
             hole = (tile, 5 * tile) if a == 0 else (0, 4 * tile)
             for place in hole:
                 tiles[layer, a * tile:(a + 1) * tile, place:place + tile] = jnp.zeros(
@@ -182,14 +182,12 @@
     tile_copies = {}
 
     def send_tiles(layer):
-        tile_copies[layer] = []
+        tile_copies[layer] = send(pieces.at[layer], arrived.at[layer], {"band": other})
+
+    def place_tiles(layer):
+        tile_copies[layer].wait_recv()
         for a in range(FACE):
-            for start, place, size in spans(a):
-                tile_copies[layer].append(send(
-                    pieces.at[layer * FACE + a, :, pl.ds(start, size)],
-                    tiles.at[layer, pl.ds(pl.multiple_of(a * tile + mine, part), part), pl.ds(place, size)],
-                    {"band": other},
-                ))
+            put(layer, a, other, arrived[layer, a])
 
     def send_halo(k, c, up):
         if up:
@@ -243,19 +241,20 @@
             halos.setdefault((k + 1, c), []).append(send_halo(k + 1, c, layer != 0))
 
     for layer in outer:
-        for copy in tile_copies[layer]:
-            copy.wait_recv()
+        place_tiles(layer)
         for c in range(chunks):
             outer_layer(0, c, layer)
     for layer in inner_layers:
-        for copy in tile_copies[layer]:
-            copy.wait_recv()
+        place_tiles(layer)
         for c in range(chunks):
             apply_layer(0, c, layer)
     for k in range(1, 4):
         for c in range(chunks):
             for layer in inner_layers:
                 apply_layer(k, c, layer)
+        if k == 3:
+            for c in range(chunks):
+                slab_t[c] = ext3[c, face:face + rows, :].T
         for c in range(chunks):
             for layer in outer:
                 outer_layer(k, c, layer)
@@ -267,15 +266,12 @@
                     send_strip(4, c, own_applied, 0)
                 keep_strip(4, c, own_applied, 0)
 
-    def transposed_dot(left, right):
-        return lax.dot_general(
-            left, right, (((0,), (0,)), ((), ())), preferred_element_type=jnp.float32
-        )
-
     def unit_start(unit, left, right):
-        to_core[unit] = transposed_dot(left(1 - core), right).astype(jnp.bfloat16)
+        to_core[unit] = jnp.dot(
+            left(1 - core), right, preferred_element_type=jnp.float32
+        ).astype(jnp.bfloat16)
         copy = send(to_core.at[unit], from_core.at[unit], sibling)
-        own32[unit] = transposed_dot(left(core), right)
+        own32[unit] = jnp.dot(left(core), right, preferred_element_type=jnp.float32)
         return copy
 
     def unit_spread(unit, copy, place, first, plane):
@@ -318,7 +314,7 @@
     cross = [2 * chunks + c for c in range(chunks)]
 
     starts = [
-        unit_start(diag[c], lambda d: ext3[d, face:face + rows, :], own_applied[c])
+        unit_start(diag[c], lambda d: slab_t[d], own_applied[c])
         for c in range(chunks)
     ]
     diag_pieces = [
@@ -326,8 +322,9 @@
     ]
     for c in range(chunks):
         strip_copies[3, c].wait_recv()
+        other_t[c] = strip3[other * chunks + c].T
     starts = [
-        unit_start(near[c], lambda d: strip3[other * chunks + d], strip4[band * chunks + c])
+        unit_start(near[c], lambda d: other_t[d], strip4[band * chunks + c])
         for c in range(chunks)
     ]
     near_pieces = [
@@ -365,7 +362,9 @@
 
     def cross_unit(c, first, plane):
         strip_copies[4, c].wait_recv()
-        start = unit_start(cross[c], lambda d: strip3[band * chunks + d], strip4[other * chunks + c])
+        start = unit_start(
+            cross[c], lambda d: slab_t[d, :, pl.ds(mine_at, strip)], strip4[other * chunks + c]
+        )
         return unit_spread(cross[c], start, place_of(c, 2), first, plane)
 
     cross_copies = {c: cross_unit(c, 1, band) for c in range(last)}
@@ -458,7 +457,7 @@
     piece = width // chips
     units = 3 * CHUNKS
     gram_scale = 1.0 / math.sqrt(float(rows * slabs) * float(bands * 2))
-    copies = 2 * blocks + 8 * CHUNKS + 2 * CHUNKS + units * (chips + 1) + 4 * depth + 5
+    copies = layers + 8 * CHUNKS + 2 * CHUNKS + units * (chips + 1) + 4 * depth + 5
     copies += CHUNKS * (4 * depth + 4)
     half = jnp.bfloat16
     flops = 2 * rows * 6 * tile * bands * 4 + 2 * 2 * strip * 4 * bands * bands
@@ -474,8 +473,11 @@
         scratch_shapes=[
             pltpu.SMEM((blocks, slots), jnp.int32),
             pltpu.VMEM((blocks, slots, part, tile), half),
-            pltpu.VMEM((blocks, part, 4 * tile), half),
+            pltpu.VMEM((layers, FACE, part, 4 * tile), half),
+            pltpu.VMEM((layers, FACE, part, 4 * tile), half),
             pltpu.VMEM((layers, face, 3 * face), half),
+            pltpu.VMEM((CHUNKS, width, rows), half),
+            pltpu.VMEM((CHUNKS, width, strip), half),
             *[pltpu.VMEM((CHUNKS, rows + 2 * face, width), half) for _ in range(4)],
             pltpu.VMEM((CHUNKS, rows, width), half),
             pltpu.VMEM((groups, strip, width), half),
@@ -493,7 +495,7 @@
             pltpu.SemaphoreType.DMA((copies,)),
         ],
         compiler_params=pltpu.CompilerParams(
-            collective_id=0, has_side_effects=True, vmem_limit_bytes=63 * 1024 * 1024 + 512 * 1024
+            collective_id=0, has_side_effects=True, vmem_limit_bytes=62 * 1024 * 1024 + 768 * 1024
         ),
         cost_estimate=pl.CostEstimate(flops=flops, bytes_accessed=4 * rows * bands, transcendentals=0),
     )(neighbors, hamiltonian, orbitals)

time: 83 us -> 82.7 us (level)
  no operation moved by 1% of the time
where the time goes in v5:
time: 82.7 us; the launch traced here: 82.6 us
  Pallas kernels  80.3 us (97%)
  local copies, waits for them, and re-layouts  2.26 us (3%)
    pallas_call x1, Pallas kernels, fused_body(): pl.pallas_call(functools.partial(kernel, slabs, gram_scale), out_shape=ja...  80.3 us
    unnamed x1, local copies, waits for them, and re-layouts  2.26 us

profile of v5, /device:TPU:1, one launch (start us, length us, event | category | flops | bytes accessed | tf_op | source)
XLA Modules:
  0.0 82.6 jit_solution(15272613300104675921)
XLA Ops:
  0.0 80.3 %shard_map.37 = bf16[512,1024]{1,0:T(8,128)(2,1)} custom-call(s32[8,7]{1,0:T(8,128)} %neighbors_ref.1, bf16[8,7,64,128]{3,2,1,0:T(8,128)(2,1)} %hamiltonian_ref.1, bf16[1024,512]{1,0:T(8,128)(2,1)} %orbitals_ref.1), custom_call_target="tpu_custom_call" | custom-call | flops 5368709120 | bytes 2097152 | tf_op jit(solution)/shard_map/pallas_call | solution.py:464
  80.3 2.3 %copy.5 = bf16[512,1024]{1,0:T(8,128)(2,1)} copy(bf16[512,1024]{1,0:T(8,128)(2,1)} %shard_map.37) | data formatting | bytes 2097152

commit v6 on v5

--- a/solution.py
+++ b/solution.py
@@ -223,12 +223,23 @@
     mine_at = pl.multiple_of(band * strip, strip)
     theirs_at = pl.multiple_of(other * strip, strip)
 
-    def send_strip(which, c, source, base):
-        place = strip3 if which == 3 else strip4
-        group = band * chunks + c
-        strip_copies[which, c] = send(
-            source.at[c, pl.ds(base + theirs_at, strip)], place.at[group], {"band": other}
-        )
+    def send_strip(c):
+        strip_copies[4, c] = [send(
+            own_applied.at[c, pl.ds(theirs_at, strip)], strip4.at[band * chunks + c], {"band": other}
+        )]
+
+    def send_part(c, source, place, size):
+        strip_copies.setdefault((3, c), []).append(send(
+            ext3.at[c, pl.ds(pl.multiple_of(face + source, face), size)],
+            strip3.at[band * chunks + c, pl.ds(pl.multiple_of(place, face), size)],
+            {"band": other},
+        ))
+
+    def send_inner(c):
+        send_part(c, other * strip + band * face, band * face, strip - face)
+
+    def send_outer(c):
+        send_part(c, other * (rows - face), other * (strip - face), face)
 
     def keep_strip(which, c, source, base):
         place = strip3 if which == 3 else strip4
@@ -252,6 +263,8 @@
         for c in range(chunks):
             for layer in inner_layers:
                 apply_layer(k, c, layer)
+            if k == 2:
+                send_inner(c)
         if k == 3:
             for c in range(chunks):
                 slab_t[c] = ext3[c, face:face + rows, :].T
@@ -259,11 +272,11 @@
             for layer in outer:
                 outer_layer(k, c, layer)
             if k == 2:
-                send_strip(3, c, ext3, face)
+                send_outer(c)
                 keep_strip(3, c, ext3, face)
             if k == 3:
                 if c < chunks - 1:
-                    send_strip(4, c, own_applied, 0)
+                    send_strip(c)
                 keep_strip(4, c, own_applied, 0)
 
     def unit_start(unit, left, right):
@@ -321,7 +334,8 @@
         unit_spread(diag[c], starts[c], place_of(c, 0), 1, band) for c in range(chunks)
     ]
     for c in range(chunks):
-        strip_copies[3, c].wait_recv()
+        for copy in strip_copies[3, c]:
+            copy.wait_recv()
         other_t[c] = strip3[other * chunks + c].T
     starts = [
         unit_start(near[c], lambda d: other_t[d], strip4[band * chunks + c])
@@ -345,7 +359,7 @@
 
     whole = (0, chunks)
     across = pass_on(own_diag, chip, at_chip(chip, other), whole)
-    send_strip(4, last, own_applied, 0)
+    send_strip(last)
     diag_levels, diag_sides = [], []
 
     def spread_diag(quad):
@@ -361,7 +375,8 @@
     spread_diag(own_diag)
 
     def cross_unit(c, first, plane):
-        strip_copies[4, c].wait_recv()
+        for copy in strip_copies[4, c]:
+            copy.wait_recv()
         start = unit_start(
             cross[c], lambda d: slab_t[d, :, pl.ds(mine_at, strip)], strip4[other * chunks + c]
         )
@@ -412,14 +427,10 @@
             plane_copies[c] += spread_plane(level_chip(depth - j), span)
 
     def mix(gr, gc, c):
-        block = gram16[(gr * 2 + gc) * chunks + c]
-        total = jnp.zeros((strip, width), jnp.float32)
-        for d in range(chunks):
-            total += jnp.dot(
-                strip3[gr * chunks + d], block[d * width:(d + 1) * width],
-                preferred_element_type=jnp.float32,
-            )
-        return total
+        left = jnp.concatenate([strip3[gr * chunks + d] for d in range(chunks)], axis=1)
+        return jnp.dot(
+            left, gram16[(gr * 2 + gc) * chunks + c], preferred_element_type=jnp.float32
+        )
 
     for copy in early_copies:
         copy.wait_recv()
@@ -457,7 +468,7 @@
     piece = width // chips
     units = 3 * CHUNKS
     gram_scale = 1.0 / math.sqrt(float(rows * slabs) * float(bands * 2))
-    copies = layers + 8 * CHUNKS + 2 * CHUNKS + units * (chips + 1) + 4 * depth + 5
+    copies = layers + 8 * CHUNKS + 3 * CHUNKS + units * (chips + 1) + 4 * depth + 5
     copies += CHUNKS * (4 * depth + 4)
     half = jnp.bfloat16
     flops = 2 * rows * 6 * tile * bands * 4 + 2 * 2 * strip * 4 * bands * bands

time: 82.7 us -> 82.7 us (level)
  no operation moved by 1% of the time
where the time goes in v6:
time: 82.7 us; the launch traced here: 82.5 us
  Pallas kernels  80.3 us (97%)
  local copies, waits for them, and re-layouts  2.26 us (3%)
    pallas_call x1, Pallas kernels, fused_body(): pl.pallas_call(functools.partial(kernel, slabs, gram_scale), out_shape=ja...  80.3 us
    unnamed x1, local copies, waits for them, and re-layouts  2.26 us

profile of v6, /device:TPU:1, one launch (start us, length us, event | category | flops | bytes accessed | tf_op | source)
XLA Modules:
  0.0 82.5 jit_solution(10383496448897612510)
XLA Ops:
  0.0 80.3 %shard_map.37 = bf16[512,1024]{1,0:T(8,128)(2,1)} custom-call(s32[8,7]{1,0:T(8,128)} %neighbors_ref.1, bf16[8,7,64,128]{3,2,1,0:T(8,128)(2,1)} %hamiltonian_ref.1, bf16[1024,512]{1,0:T(8,128)(2,1)} %orbitals_ref.1), custom_call_target="tpu_custom_call" | custom-call | flops 5368709120 | bytes 2097152 | tf_op jit(solution)/shard_map/pallas_call | solution.py:475
  80.3 2.3 %copy.5 = bf16[512,1024]{1,0:T(8,128)(2,1)} copy(bf16[512,1024]{1,0:T(8,128)(2,1)} %shard_map.37) | data formatting | bytes 2097152

commit v7 on v6

--- a/solution.py
+++ b/solution.py
@@ -76,7 +76,7 @@
 def kernel(
     slabs, gram_scale, neighbors_ref, hamiltonian_ref, orbitals_ref, out_ref,
     names, slots, pieces, arrived, tiles, slab_t, other_t, ext0, ext1, ext2, ext3, own_applied, strip3, strip4, own32, to_core, from_core,
-    to_peers, from_peers, crossing, gram16, out32, local_sem, send_sem, recv_sem,
+    to_peers, from_peers, to_side, from_side, to_level, crossing, gram16, out32, local_sem, send_sem, recv_sem,
 ):
     slab, band = lax.axis_index("slab"), lax.axis_index("band")
     other = 1 - band
@@ -300,10 +300,39 @@
             ))
         return copies
 
+    beside = level * 2 + (1 - column)
+
+    def level_chip(offset):
+        return lax.rem(level + offset, depth) * 2 + column
+
+    def side_start(unit, copy):
+        copy.wait_recv()
+        own32[unit] = own32[unit] + from_core[unit].astype(jnp.float32)
+        for z in range(depth):
+            row = pl.multiple_of((z * 2 + 1 - column) * piece, piece)
+            to_side[unit, z] = own32[unit, pl.ds(row, piece), :].astype(jnp.bfloat16)
+        return send(to_side.at[unit], from_side.at[unit], at_chip(beside, band))
+
+    def level_start(unit, copy, place):
+        copy.wait_recv()
+        for z in range(depth):
+            row = pl.multiple_of((z * 2 + column) * piece, piece)
+            to_level[unit, z] = (
+                own32[unit, pl.ds(row, piece), :] + from_side[unit, z].astype(jnp.float32)
+            ).astype(jnp.bfloat16)
+        return [
+            send(
+                to_level.at[unit, lax.rem(level + j, depth)],
+                from_peers.at[place + j],
+                at_chip(level_chip(j), band),
+            )
+            for j in range(1, depth)
+        ]
+
     my_piece = pl.multiple_of(chip * piece, piece)
 
     def piece_sum(unit, places):
-        total = to_peers[unit, pl.ds(my_piece, piece), :].astype(jnp.float32)
+        total = to_level[unit, level].astype(jnp.float32)
         for place in places:
             total = total + from_peers[place].astype(jnp.float32)
         return total
@@ -330,9 +359,8 @@
         unit_start(diag[c], lambda d: slab_t[d], own_applied[c])
         for c in range(chunks)
     ]
-    diag_pieces = [
-        unit_spread(diag[c], starts[c], place_of(c, 0), 1, band) for c in range(chunks)
-    ]
+    sides = [side_start(diag[c], starts[c]) for c in range(chunks)]
+    diag_pieces = [level_start(diag[c], sides[c], place_of(c, 0)) for c in range(chunks)]
     for c in range(chunks):
         for copy in strip_copies[3, c]:
             copy.wait_recv()
@@ -341,21 +369,16 @@
         unit_start(near[c], lambda d: other_t[d], strip4[band * chunks + c])
         for c in range(chunks)
     ]
-    near_pieces = [
-        unit_spread(near[c], starts[c], place_of(c, 1), 1, band) for c in range(chunks)
-    ]
-
-    def level_chip(offset):
-        return lax.rem(level + offset, depth) * 2 + column
-
-    beside = level * 2 + (1 - column)
+    sides = [side_start(near[c], starts[c]) for c in range(chunks)]
+    near_pieces = [level_start(near[c], sides[c], place_of(c, 1)) for c in range(chunks)]
+
     own_diag, other_diag = band * 3, other * 3
     own_off, other_off = other * 2 + band, band * 2 + other
 
     for c in range(chunks):
         for copy in diag_pieces[c]:
             copy.wait_recv()
-        summed(diag[c], [place_of(c, 0) + j for j in range(1, chips)], own_diag, c)
+        summed(diag[c], [place_of(c, 0) + j for j in range(1, depth)], own_diag, c)
 
     whole = (0, chunks)
     across = pass_on(own_diag, chip, at_chip(chip, other), whole)
@@ -374,27 +397,29 @@
 
     spread_diag(own_diag)
 
-    def cross_unit(c, first, plane):
+    def cross_start(c):
         for copy in strip_copies[4, c]:
             copy.wait_recv()
-        start = unit_start(
+        return unit_start(
             cross[c], lambda d: slab_t[d, :, pl.ds(mine_at, strip)], strip4[other * chunks + c]
         )
-        return unit_spread(cross[c], start, place_of(c, 2), first, plane)
-
-    cross_copies = {c: cross_unit(c, 1, band) for c in range(last)}
+
+    cross_copies = {}
+    for c in range(last):
+        side = side_start(cross[c], cross_start(c))
+        cross_copies[c] = level_start(cross[c], side, place_of(c, 2))
     across.wait_recv()
     spread_diag(other_diag)
     for c in range(last):
         for copy in cross_copies[c]:
             copy.wait_recv()
-        total = piece_sum(cross[c], [place_of(c, 2) + j for j in range(1, chips)])
+        total = piece_sum(cross[c], [place_of(c, 2) + j for j in range(1, depth)])
         crossing[c] = total.astype(jnp.bfloat16)
         cross_copies[c] = [send(crossing.at[c], from_peers.at[place_of(c, 2)], at_chip(chip, other))]
     for quad, j, copy in diag_levels:
         copy.wait_recv()
         diag_sides.append(pass_on(quad, level_chip(depth - j), at_chip(beside, band), whole))
-    cross_copies[last] = cross_unit(last, 0, other)
+    cross_copies[last] = unit_spread(cross[last], cross_start(last), place_of(last, 2), 0, other)
     for copy in diag_sides:
         copy.wait_recv()
     early_copies = [block_to_sibling(quad, whole) for quad in (own_diag, other_diag)]
@@ -402,7 +427,7 @@
     def sum_off(c):
         for copy in near_pieces[c] + cross_copies[c]:
             copy.wait_recv()
-        places = [place_of(c, 1) + j for j in range(1, chips)]
+        places = [place_of(c, 1) + j for j in range(1, depth)]
         places += [place_of(c, 2) + j for j in range(chips if c == last else 1)]
         summed(near[c], places, own_off, c)
 
@@ -498,6 +523,7 @@
             pltpu.VMEM((units, width, width), half),
             pltpu.VMEM((units, width, width), half),
             pltpu.VMEM((units * chips, piece, width), half),
+            *[pltpu.VMEM((units, depth, piece, width), half) for _ in range(3)],
             pltpu.VMEM((CHUNKS, piece, width), half),
             pltpu.VMEM((4 * CHUNKS, CHUNKS * width, width), half),
             pltpu.VMEM((groups, strip, width), jnp.float32),

time: 82.7 us -> 82.2 us (level)
  no operation moved by 1% of the time
where the time goes in v7:
time: 82.2 us; the launch traced here: 82.1 us
  Pallas kernels  79.8 us (97%)
  local copies, waits for them, and re-layouts  2.26 us (3%)
    pallas_call x1, Pallas kernels, fused_body(): pl.pallas_call(functools.partial(kernel, slabs, gram_scale), out_shape=ja...  79.8 us
    unnamed x1, local copies, waits for them, and re-layouts  2.26 us

profile of v7, /device:TPU:1, one launch (start us, length us, event | category | flops | bytes accessed | tf_op | source)
XLA Modules:
  0.0 82.1 jit_solution(15809457131657984685)
XLA Ops:
  0.0 79.8 %shard_map.37 = bf16[512,1024]{1,0:T(8,128)(2,1)} custom-call(s32[8,7]{1,0:T(8,128)} %neighbors_ref.1, bf16[8,7,64,128]{3,2,1,0:T(8,128)(2,1)} %hamiltonian_ref.1, bf16[1024,512]{1,0:T(8,128)(2,1)} %orbitals_ref.1), custom_call_target="tpu_custom_call" | custom-call | flops 5368709120 | bytes 2097152 | tf_op jit(solution)/shard_map/pallas_call | solution.py:500
  79.8 2.3 %copy.5 = bf16[512,1024]{1,0:T(8,128)(2,1)} copy(bf16[512,1024]{1,0:T(8,128)(2,1)} %shard_map.37) | data formatting | bytes 2097152
